TPU v7x, 256 devices: a whole 4x4x8 slice. The times are simulated.
256 devices in a mesh: cloud: 8 (over y_lo, x), leaf: 32 (over y_hi, z, core).
Axes of the slice: x: 4, y: 4 (y_hi: 2, y_lo: 2; y = y_hi * 2 + y_lo), z: 8, core: 2. Of those that a mesh axis runs over, the one named last changes fastest.
Arguments:
- points: bfloat16 [262144, 512], P(('cloud', 'leaf')), parts along dimension 0
- tree_order: int32 [262144], P(('cloud', 'leaf')), parts along dimension 0, may hold values from 0 to 1023, as said below
- present: int32 [262144], P(('cloud', 'leaf')), parts along dimension 0, may hold values 0 or 1
- gain_attn: float32 [3, 512], replicated, may hold values from 0.1 to 1.9
- query_weight: bfloat16 [3, 512, 512], replicated
- key_weight: bfloat16 [3, 512, 512], replicated
- value_weight: bfloat16 [3, 512, 512], replicated, may hold values from -0.25 to 0.25
- out_weight: bfloat16 [3, 512, 512], replicated, may hold values from -0.25 to 0.25
- gain_mlp: float32 [512], replicated, may hold values from 0.1 to 1.9
- hidden_weight: bfloat16 [512, 2048], replicated, may hold values from -0.25 to 0.25
- proj_weight: bfloat16 [2048, 512], replicated, may hold values from -0.125 to 0.125
Outputs:
- field: bfloat16 [262144, 512], P(('cloud', 'leaf')), parts along dimension 0
There are 8 independent parts, one for each index of `cloud`. A program takes and returns all parts, laid end to end along the dimension named above; an argument that names none is the same for every part. Nothing has to cross between parts.
Inputs may be any that keep to these rules, and one draw needn't show every extreme that they name: `tree_order`: within each aligned block of 1024 entries, each of 0 to 1023 appears once.
All inputs are finite; a program needn't handle non-finite values. No bound on the sum of `present` on one device may be relied on, other than what follows from the above.
Results may differ from a plain program's by a relative error of at most 0.025.
Values may be sent and summed in bfloat16 or wider, within the bound.
No kernel may reach another device: no remote copies, remote signals or barrier semaphores. Data moves between devices by JAX's collectives and lax.ppermute only.
A program may use at most 192 MiB of HBM per device.

v0:
```python
import jax
import jax.numpy as jnp
from jax import lax
from jax.sharding import PartitionSpec as P

HEAD = 64


def partner(value, axis, bit):
    mask = 2**bit
    pairs = [(source, source ^ mask) for source in range(lax.axis_size(axis))]
    return lax.ppermute(value, axis, pairs)


def norm_rows(values, gain_row):
    wide = values.astype(jnp.float32)
    centre = jnp.mean(wide, axis=-1, keepdims=True)
    spread = jnp.mean(jnp.square(wide - centre), axis=-1, keepdims=True)
    return ((wide - centre) * lax.rsqrt(spread + 1e-05) * gain_row).astype(jnp.bfloat16)


def product(values, weight):
    return jnp.dot(values, weight, preferred_element_type=jnp.float32)


def attend(queries, key_rows, value_rows, key_filled):
    row_count = queries.shape[0]
    model_width = queries.shape[1]
    head_count = model_width // HEAD
    query_heads = queries.reshape(row_count, head_count, HEAD)
    key_heads = key_rows.reshape(-1, head_count, HEAD)
    value_heads = value_rows.reshape(-1, head_count, HEAD)
    scores = jnp.einsum(
        "qhd,khd->hqk", query_heads, key_heads, preferred_element_type=jnp.float32
    ) * HEAD ** (-0.5)
    own_row = (
        jnp.arange(key_rows.shape[0], dtype=jnp.int32)[None, :]
        == jnp.arange(row_count, dtype=jnp.int32)[:, None]
    )
    allowed = (key_filled[None, :] > 0) | own_row
    scores = jnp.where(allowed[None], scores, -1e30)
    row_top = jnp.max(scores, axis=-1, keepdims=True)
    weights = jnp.exp(scores - row_top)
    weights = (weights / jnp.sum(weights, axis=-1, keepdims=True)).astype(jnp.bfloat16)
    merged = jnp.einsum("hqk,khd->qhd", weights, value_heads, preferred_element_type=jnp.float32)
    return merged.reshape(row_count, model_width).astype(jnp.bfloat16)


def trade_pairs(key_rows, value_rows, filled, level_index, base_bit):
    if level_index == 0:
        return partner((key_rows, value_rows, filled), "leaf", base_bit)
    if level_index == 1:
        return partner((key_rows, value_rows, filled), "leaf", base_bit + 1)
    return partner((key_rows, value_rows, filled), "leaf", base_bit + 2)


def per_device(
    points,
    tree_order,
    present,
    gain_attn,
    query_weight,
    key_weight,
    value_weight,
    out_weight,
    gain_mlp,
    hidden_weight,
    proj_weight,
):
    base_bit = lax.axis_size("leaf").bit_length() - 1 - 3
    filled = present[tree_order].astype(jnp.bfloat16)
    current = points[tree_order] * filled[:, None]
    skips = []
    for level_index in range(3):
        normed = norm_rows(current, gain_attn[level_index])
        queries = product(normed, query_weight[level_index]).astype(jnp.bfloat16)
        key_rows = product(normed, key_weight[level_index]).astype(jnp.bfloat16)
        value_rows = product(normed, value_weight[level_index]).astype(jnp.bfloat16)
        far_keys, far_values, far_filled = trade_pairs(
            key_rows, value_rows, filled, level_index, base_bit
        )
        joined_keys = jnp.concatenate([key_rows, far_keys], axis=0)
        joined_values = jnp.concatenate([value_rows, far_values], axis=0)
        joined_filled = jnp.concatenate([filled, far_filled], axis=0)
        attended = attend(queries, joined_keys, joined_values, joined_filled)
        current = (current.astype(jnp.float32) + product(attended, out_weight[level_index])).astype(
            jnp.bfloat16
        )
        if level_index < 2:
            skips.append(current)
            rows_now = current.shape[0]
            model_width = current.shape[1]
            current = jnp.mean(
                current.reshape(rows_now // 2, 2, model_width).astype(jnp.float32), axis=1
            ).astype(jnp.bfloat16)
            filled = jnp.max(filled.reshape(rows_now // 2, 2), axis=1)
    normed = norm_rows(current, gain_mlp)
    hidden = jax.nn.gelu(product(normed, hidden_weight), approximate=True).astype(jnp.bfloat16)
    current = (current.astype(jnp.float32) + product(hidden, proj_weight)).astype(jnp.bfloat16)
    for skip_rows in reversed(skips):
        spread_rows = jnp.repeat(current, 2, axis=0)
        current = (skip_rows.astype(jnp.float32) + spread_rows.astype(jnp.float32)).astype(
            jnp.bfloat16
        )
    return jnp.zeros_like(current).at[tree_order].set(current)


def solution(mesh):
    placed = (
        P(("cloud", "leaf"), None),
        P(("cloud", "leaf")),
        P(("cloud", "leaf")),
        P(),
        P(),
        P(),
        P(),
        P(),
        P(),
        P(),
        P(),
    )
    return jax.shard_map(
        per_device,
        mesh=mesh,
        in_specs=placed,
        out_specs=P(("cloud", "leaf"), None),
        check_vma=False,
    )
```

profile of v0, /device:TPU:18, one launch (start us, length us, event | category | flops | bytes accessed | tf_op | source)
XLA Modules:
  0.0 327.4 jit_solution(9164927748752581562)
XLA Ops:
  0.0 1.4 broadcast_clamp_fusion
  1.4 4.5 %gather_fusion.1 = s32[1024]{0:T(1024)S(1)} fusion(s32[1024]{0:T(1024)S(1)} %copy-done.1, s32[1024]{0:T(1024)S(1)} %get-tuple-element.12), kind=kCustom, calls=%fused_computation.1 | custom fusion | bytes 12288 | tf_op jit(solution)/shard_map/gather | solution.py:71
  6.0 3.4 %collective-permute-start.1 = (bf16[1024]{0:T(1024)(128)(2,1)S(1)}, bf16[1024]{0:T(1024)(128)(2,1)S(1)}, u32[]{:S(2)}, u32[]{:S(2)}) collective-permute-start(bf16[1024]{0:T(1024)(128)(2,1)S(1)} %convert_element_type.163), channel_id=1, source_target_pairs={{0,4},{1,5},{2,6},{3,7},{4,0},{5,1},{6,2},{7,3},{8,12},{9,13},{10,... | collective-permute-start | bytes 6152 | tf_op jit(solution)/shard_map/ppermute | solution.py:12
  9.3 5.1 %gather_fusion = bf16[1024,512]{1,0:T(8,128)(2,1)} fusion(bf16[1024,512]{1,0:T(8,128)(2,1)S(1)} %copy-done.2, s32[1024]{0:T(1024)S(1)} %get-tuple-element.12), kind=kCustom, calls=%fused_computation | custom fusion | bytes 2101248 | tf_op jit(solution)/shard_map/gather | solution.py:72
  14.4 1.7 convert_reduce_fusion
  16.2 1.9 fusion.19
  19.2 3.2 convolution_convert_fusion
  22.4 2.7 convolution_convert_fusion.2
  25.1 2.9 collective-permute-start
  28.4 5.5 %collective-permute-start.4 = (bf16[512]{0:T(512)(128)(2,1)S(1)}, bf16[512]{0:T(512)(128)(2,1)S(1)}, u32[]{:S(2)}, u32[]{:S(2)}) collective-permute-start(bf16[512]{0:T(512)(128)(2,1)S(1)} %reduce_max.46), channel_id=1, source_target_pairs={{0,8},{1,9},{2,10},{3,11},{4,12},{5,13},{6,14},{7,15},{8,0},{9,1},... | collective-permute-start | bytes 3080 | tf_op jit(solution)/shard_map/ppermute | solution.py:12
  34.2 0.9 collective-permute-start.7
  35.1 3.1 convolution_convert_fusion.1
  38.2 1.6 collective-permute-done.7
  39.8 0.7 fusion.87
  40.5 34.2 %collective-permute-done.4 = bf16[512]{0:T(512)(128)(2,1)S(1)} collective-permute-done((bf16[512]{0:T(512)(128)(2,1)S(1)}, bf16[512]{0:T(512)(128)(2,1)S(1)}, u32[]{:S(2)}, u32[]{:S(2)}) %collective-permute-start.4) | collective-permute-done | bytes 1056 | tf_op jit(solution)/shard_map/ppermute | solution.py:12
  74.7 2.4 fusion.11
  77.0 17.6 %collective-permute-done.2 = bf16[1024,512]{1,0:T(8,128)(2,1)} collective-permute-done((bf16[1024,512]{1,0:T(8,128)(2,1)}, bf16[1024,512]{1,0:T(8,128)(2,1)}, u32[]{:S(2)}, u32[]{:S(2)}) %collective-permute-start.2) | collective-permute-done | bytes 1048608 | tf_op jit(solution)/shard_map/ppermute | solution.py:12
  94.6 3.0 pad_maximum_fusion.1
  97.7 4.0 %copy.20 = bf16[2048,512]{0,1:T(8,128)(2,1)} copy(bf16[2048,512]{1,0:T(8,128)(2,1)} %pad_maximum_fusion.1) | data formatting | bytes 4194304 | tf_op jit(solution)/shard_map/concatenate | solution.py:82
  101.7 14.0 %collective-permute-done = bf16[1024,512]{1,0:T(8,128)(2,1)} collective-permute-done((bf16[1024,512]{1,0:T(8,128)(2,1)}, bf16[1024,512]{1,0:T(8,128)(2,1)}, u32[]{:S(2)}, u32[]{:S(2)}) %collective-permute-start) | collective-permute-done | bytes 1048608 | tf_op jit(solution)/shard_map/ppermute | solution.py:12
  115.6 3.0 pad_maximum_fusion
  118.7 4.0 %copy.19 = bf16[2048,512]{0,1:T(8,128)(2,1)} copy(bf16[2048,512]{1,0:T(8,128)(2,1)} %pad_maximum_fusion) | data formatting | bytes 4194304 | tf_op jit(solution)/shard_map/concatenate | solution.py:83
  122.7 30.5 %fusion.116 = (f32[8,1024]{1,0:T(8,128)S(1)}, f32[8,1024,2048]{2,1,0:T(8,128)}) fusion(pred[1024,2048]{1,0:T(8,128)(4,1)} %fusion.11, bf16[1024,8,64]{0,2,1:T(8,128)(2,1)} %bitcast.98, bf16[2048,8,64]{0,2,1:T(8,128)(2,1)} %bitcast.82), kind=kOutput, calls=%fused_computation.163 | convolution fusion | flops 2214594560 | bytes 72384512 | tf_op jit(solution)/shard_map/sub | solution.py:43
  153.2 24.7 %fusion.37 = bf16[8,64,1024]{2,1,0:T(8,128)(2,1)} fusion(bf16[2048,8,64]{0,2,1:T(8,128)(2,1)} %bitcast.83, f32[8,1024,2048]{2,1,0:T(8,128)} %get-tuple-element.15, f32[8,1024]{1,0:T(8,128)S(1)} %get-tuple-element.14), kind=kOutput, calls=%fused_computation.63 | convolution fusion | flops 2181562368 | bytes 70287360 | tf_op jit(solution)/shard_map/hqk,khd->qhd/dot_general | solution.py:45
  177.9 3.5 %fusion.36 = f32[1024,512]{1,0:T(8,128)} fusion(bf16[1024,512]{0,1:T(8,128)(2,1)} %bitcast.99, bf16[1024,512]{1,0:T(8,128)(2,1)S(1)} %copy-done.3, bf16[3,512,512]{2,1,0:T(8,128)(2,1)} %param.18, bf16[1024]{0:T(1024)(128)(2,1)S(1)} %convert_element_type.163), kind=kOutput, calls=%fused_computation.59 | convolution fusion | flops 539492352 | bytes 4720640 | tf_op jit(solution)/shard_map/dot_general | solution.py:23
  181.3 3.7 %reshape.245 = f32[512,2,512]{2,1,0:T(2,128)} reshape(f32[1024,512]{1,0:T(8,128)} %fusion.36) | data formatting | bytes 4194304 | tf_op jit(solution)/shard_map/convert_element_type | solution.py:94
  185.0 4.1 %reduce_sum.120 = f32[512,512]{1,0:T(8,128)S(1)} reduce(f32[512,2,512]{2,1,0:T(2,128)} %reshape.245, f32[]{:T(128)} %constant.17.clone.1), dimensions={1}, to_apply=%region_4.5 | reduce | flops 262144 | bytes 3145732 | tf_op jit(solution)/shard_map/reduce_sum | solution.py:93
  189.6 1.6 convolution_convert_fusion.3
  191.1 5.5 %collective-permute-start.5 = (bf16[512,512]{1,0:T(8,128)(2,1)S(1)}, bf16[512,512]{1,0:T(8,128)(2,1)S(1)}, u32[]{:S(2)}, u32[]{:S(2)}) collective-permute-start(bf16[512,512]{1,0:T(8,128)(2,1)S(1)} %convolution_convert_fusion.3), channel_id=1, source_target_pairs={{0,8},{1,9},{2,10},{3,11},{4,12},{5,13},{6,14},{7,15},{8,0},{9,1},... | collective-permute-start | bytes 1572872 | tf_op jit(solution)/shard_map/ppermute | solution.py:12
  196.6 2.3 convolution_convert_fusion.5
  199.5 1.0 fusion.33
  200.5 2.5 convolution_convert_fusion.4
  202.9 22.9 %collective-permute-done.5 = bf16[512,512]{1,0:T(8,128)(2,1)S(1)} collective-permute-done((bf16[512,512]{1,0:T(8,128)(2,1)S(1)}, bf16[512,512]{1,0:T(8,128)(2,1)S(1)}, u32[]{:S(2)}, u32[]{:S(2)}) %collective-permute-start.5) | collective-permute-done | bytes 524320 | tf_op jit(solution)/shard_map/ppermute | solution.py:12
  226.0 1.3 copy.22
  227.3 15.2 %collective-permute-done.3 = bf16[512,512]{1,0:T(8,128)(2,1)} collective-permute-done((bf16[512,512]{1,0:T(8,128)(2,1)}, bf16[512,512]{1,0:T(8,128)(2,1)}, u32[]{:S(2)}, u32[]{:S(2)}) %collective-permute-start.3) | collective-permute-done | bytes 524320 | tf_op jit(solution)/shard_map/ppermute | solution.py:12
  242.5 1.3 pad_maximum_fusion.2
  243.7 1.3 copy.21
  245.1 10.6 %fusion.117 = (f32[8,512]{1,0:T(8,128)S(1)}, f32[8,512,1024]{2,1,0:T(8,128)}) fusion(pred[512,1024]{1,0:T(8,128)(4,1)} %fusion.33, bf16[512,8,64]{0,2,1:T(8,128)(2,1)} %bitcast.100, bf16[1024,8,64]{0,2,1:T(8,128)(2,1)} %bitcast.84), kind=kOutput, calls=%fused_computation.164 | convolution fusion | flops 553649152 | bytes 18890752 | tf_op jit(solution)/shard_map/sub | solution.py:43
  255.7 8.5 %fusion.40 = bf16[8,64,512]{2,1,0:T(8,128)(2,1)S(1)} fusion(bf16[1024,8,64]{0,2,1:T(8,128)(2,1)S(1)} %bitcast.85, f32[8,512,1024]{2,1,0:T(8,128)} %get-tuple-element.17, f32[8,512]{1,0:T(8,128)S(1)} %get-tuple-element.16), kind=kOutput, calls=%fused_computation.69 | convolution fusion | flops 545521664 | bytes 18366464 | tf_op jit(solution)/shard_map/hqk,khd->qhd/dot_general | solution.py:45
  264.3 1.5 fusion.39
  265.8 1.6 reshape.246
  267.4 3.3 reduce_sum.124
  270.6 1.2 convert_reduce_fusion.2
  272.0 2.1 convolution_convert_fusion.6
  274.5 2.1 convolution_convert_fusion.8
  276.6 3.4 %collective-permute-start.6 = (bf16[256,512]{1,0:T(8,128)(2,1)}, bf16[256,512]{1,0:T(8,128)(2,1)}, u32[]{:S(2)}, u32[]{:S(2)}) collective-permute-start(bf16[256,512]{1,0:T(8,128)(2,1)} %convolution_convert_fusion.8), channel_id=1, source_target_pairs={{0,16},{1,17},{2,18},{3,19},{4,20},{5,21},{6,22},{7,23},{8,24},{9,... | collective-permute-start | bytes 786440 | tf_op jit(solution)/shard_map/ppermute | solution.py:12
  280.0 2.1 convolution_convert_fusion.7
  282.1 1.8 copy.24
  283.8 1.3 collective-permute-done.8
  285.2 1.9 pad_maximum_fusion.5
  287.1 2.0 copy.25
  289.1 1.9 pad_maximum_fusion.4
  291.0 2.1 copy.23
  293.0 4.6 %fusion.118 = (f32[8,256]{1,0:T(8,128)S(1)}, f32[8,256,512]{2,1,0:T(8,128)}) fusion(pred[256,512]{1,0:T(8,128)(4,1)S(1)} %copy-done.9, bf16[256,8,64]{0,2,1:T(8,128)(2,1)} %bitcast.89, bf16[512,8,64]{0,2,1:T(8,128)(2,1)} %bitcast.87), kind=kOutput, calls=%fused_computation.165 | convolution fusion | flops 138412544 | bytes 5120000 | tf_op jit(solution)/shard_map/sub | solution.py:43
  297.6 3.2 fusion.47
  300.8 1.5 fusion.119
  302.3 0.8 copy-done.6
  303.3 4.3 %fusion.44 = f32[256,512]{1,0:T(8,128)} fusion(f32[256,512]{1,0:T(8,128)} %copy-done.6, bf16[2048,512]{1,0:T(8,128)(2,1)S(1)} %copy-done, bf16[512,2048]{1,0:T(8,128)(2,1)} %param.20, f32[512]{0:T(512)S(1)} %copy-done.12, f32[256]{0:T(256)S(1)} %add_rsqrt_fusion.2, f32[256]{0:T(256)S(1)} %broadcast_multiply_fusion.2), kind=kOutput, calls=%fused_computation.75 | convolution fusion | flops 1079377920 | bytes 5246976 | tf_op jit(solution)/shard_map/dot_general | solution.py:23
  307.6 2.4 broadcast_in_dim.52
  310.0 2.9 convert_element_type.208
  312.9 1.4 fusion.61
  314.3 2.0 broadcast_in_dim.53
  316.3 3.7 %convert_element_type.211 = f32[1024,512]{1,0:T(8,128)} reshape(f32[512,2,512]{2,1,0:T(2,128)} %broadcast_in_dim.53) | data formatting | bytes 4194304 | tf_op jit(solution)/shard_map/convert_element_type | solution.py:102
  320.0 7.1 %scatter_custom_fusion = bf16[1024,512]{1,0:T(8,128)(2,1)} fusion(s32[1024]{0:T(1024)} %get-tuple-element.13, f32[1024,512]{1,0:T(8,128)} %fusion.36, f32[1024,512]{1,0:T(8,128)} %convert_element_type.211, bf16[]{:T(256)} %constant.14.clone.1), kind=kCustom, calls=%fused_computation.85 | custom fusion | flops 1048576 | bytes 5243392 | tf_op jit(solution)/shard_map/scatter | solution.py:105
  (53 shorter events, 3.7 us)
Async XLA Ops:
  0.0 303.3 %copy-start = (bf16[2048,512]{1,0:T(8,128)(2,1)S(1)}, bf16[2048,512]{1,0:T(8,128)(2,1)}, u32[]{:S(2)}) copy-start(bf16[2048,512]{1,0:T(8,128)(2,1)} %param.21) | copy-start | bytes 6291460
  0.0 1.4 copy-start.1
  1.4 7.9 %copy-start.2 = (bf16[1024,512]{1,0:T(8,128)(2,1)S(1)}, bf16[1024,512]{1,0:T(8,128)(2,1)}, u32[]{:S(2)}) copy-start(bf16[1024,512]{1,0:T(8,128)(2,1)} %param.11) | copy-start | bytes 3145732
  6.0 68.7 %collective-permute-start.1 = (bf16[1024]{0:T(1024)(128)(2,1)S(1)}, bf16[1024]{0:T(1024)(128)(2,1)S(1)}, u32[]{:S(2)}, u32[]{:S(2)}) collective-permute-start(bf16[1024]{0:T(1024)(128)(2,1)S(1)} %convert_element_type.163), channel_id=1, source_target_pairs={{0,4},{1,5},{2,6},{3,7},{4,0},{5,1},{6,2},{7,3},{8,12},{9,13},{10,... | collective-permute-start | bytes 6152 | tf_op jit(solution)/shard_map/ppermute | solution.py:12
  14.4 3.7 %copy-start.10 = (f32[3,512]{1,0:T(4,128)S(1)}, f32[3,512]{1,0:T(4,128)}, u32[]{:S(2)}) copy-start(f32[3,512]{1,0:T(4,128)} %param.14) | copy-start | bytes 18436
  14.4 4.3 %copy-start.3 = (bf16[1024,512]{1,0:T(8,128)(2,1)S(1)}, bf16[1024,512]{1,0:T(8,128)(2,1)}, u32[]{:S(2)}) copy-start(bf16[1024,512]{1,0:T(8,128)(2,1)} %gather_fusion) | copy-start | bytes 3145732
  19.2 5.9 %copy-start.7 = (bf16[1024,512]{1,0:T(8,128)(2,1)}, bf16[1024,512]{1,0:T(8,128)(2,1)S(1)}, u32[]{:S(2)}) copy-start(bf16[1024,512]{1,0:T(8,128)(2,1)S(1)} %fusion.21) | copy-start | bytes 3145732
  22.4 72.3 %collective-permute-start.2 = (bf16[1024,512]{1,0:T(8,128)(2,1)}, bf16[1024,512]{1,0:T(8,128)(2,1)}, u32[]{:S(2)}, u32[]{:S(2)}) collective-permute-start(bf16[1024,512]{1,0:T(8,128)(2,1)} %convolution_convert_fusion), channel_id=1, source_target_pairs={{0,4},{1,5},{2,6},{3,7},{4,0},{5,1},{6,2},{7,3},{8,12},{9,13},{10,... | collective-permute-start | bytes 3145736 | tf_op jit(solution)/shard_map/ppermute | solution.py:12
  25.1 90.5 %collective-permute-start = (bf16[1024,512]{1,0:T(8,128)(2,1)}, bf16[1024,512]{1,0:T(8,128)(2,1)}, u32[]{:S(2)}, u32[]{:S(2)}) collective-permute-start(bf16[1024,512]{1,0:T(8,128)(2,1)} %convolution_convert_fusion.2), channel_id=1, source_target_pairs={{0,4},{1,5},{2,6},{3,7},{4,0},{5,1},{6,2},{7,3},{8,12},{9,13},{10,... | collective-permute-start | bytes 3145736 | tf_op jit(solution)/shard_map/ppermute | solution.py:12
  28.4 46.2 %collective-permute-start.4 = (bf16[512]{0:T(512)(128)(2,1)S(1)}, bf16[512]{0:T(512)(128)(2,1)S(1)}, u32[]{:S(2)}, u32[]{:S(2)}) collective-permute-start(bf16[512]{0:T(512)(128)(2,1)S(1)} %reduce_max.46), channel_id=1, source_target_pairs={{0,8},{1,9},{2,10},{3,11},{4,12},{5,13},{6,14},{7,15},{8,0},{9,1},... | collective-permute-start | bytes 3080 | tf_op jit(solution)/shard_map/ppermute | solution.py:12
  34.2 5.6 %collective-permute-start.7 = (bf16[256]{0:T(256)(128)(2,1)S(1)}, bf16[256]{0:T(256)(128)(2,1)S(1)}, u32[]{:S(2)}, u32[]{:S(2)}) collective-permute-start(bf16[256]{0:T(256)(128)(2,1)S(1)} %reduce_max.48), channel_id=1, source_target_pairs={{0,16},{1,17},{2,18},{3,19},{4,20},{5,21},{6,22},{7,23},{8,24},{9,... | collective-permute-start | bytes 1544 | tf_op jit(solution)/shard_map/ppermute | solution.py:12
  189.3 11.2 %copy-start.4 = (bf16[512,512]{1,0:T(8,128)(2,1)}, bf16[512,512]{1,0:T(8,128)(2,1)S(1)}, u32[]{:S(2)}) copy-start(bf16[512,512]{1,0:T(8,128)(2,1)S(1)} %get-tuple-element.8) | copy-start | bytes 1572868
  191.1 34.8 %collective-permute-start.5 = (bf16[512,512]{1,0:T(8,128)(2,1)S(1)}, bf16[512,512]{1,0:T(8,128)(2,1)S(1)}, u32[]{:S(2)}, u32[]{:S(2)}) collective-permute-start(bf16[512,512]{1,0:T(8,128)(2,1)S(1)} %convolution_convert_fusion.3), channel_id=1, source_target_pairs={{0,8},{1,9},{2,10},{3,11},{4,12},{5,13},{6,14},{7,15},{8,0},{9,1},... | collective-permute-start | bytes 1572872 | tf_op jit(solution)/shard_map/ppermute | solution.py:12
  199.0 43.5 %collective-permute-start.3 = (bf16[512,512]{1,0:T(8,128)(2,1)}, bf16[512,512]{1,0:T(8,128)(2,1)}, u32[]{:S(2)}, u32[]{:S(2)}) collective-permute-start(bf16[512,512]{1,0:T(8,128)(2,1)} %convolution_convert_fusion.5), channel_id=1, source_target_pairs={{0,8},{1,9},{2,10},{3,11},{4,12},{5,13},{6,14},{7,15},{8,0},{9,1},... | collective-permute-start | bytes 1572872 | tf_op jit(solution)/shard_map/ppermute | solution.py:12
  245.1 10.6 %copy-start.8 = (bf16[1024,512]{0,1:T(8,128)(2,1)S(1)}, bf16[1024,512]{0,1:T(8,128)(2,1)}, u32[]{:S(2)}) copy-start(bf16[1024,512]{0,1:T(8,128)(2,1)} %copy.21) | copy-start | bytes 3145732
  255.7 8.6 %copy-start.5 = (bf16[512,512]{1,0:T(8,128)(2,1)S(1)}, bf16[512,512]{1,0:T(8,128)(2,1)}, u32[]{:S(2)}) copy-start(bf16[512,512]{1,0:T(8,128)(2,1)} %copy-done.4) | copy-start | bytes 1572868
  265.8 6.3 %copy-start.11 = (f32[1,512]{1,0:T(1,128)S(1)}, f32[1,512]{1,0:T(1,128)}, u32[]{:S(2)}) copy-start(f32[1,512]{1,0:T(1,128)} %get-tuple-element.9) | copy-start | bytes 6148
  274.1 11.1 %collective-permute-start.8 = (bf16[256,512]{1,0:T(8,128)(2,1)}, bf16[256,512]{1,0:T(8,128)(2,1)}, u32[]{:S(2)}, u32[]{:S(2)}) collective-permute-start(bf16[256,512]{1,0:T(8,128)(2,1)} %convolution_convert_fusion.6), channel_id=1, source_target_pairs={{0,16},{1,17},{2,18},{3,19},{4,20},{5,21},{6,22},{7,23},{8,24},{9,... | collective-permute-start | bytes 786440 | tf_op jit(solution)/shard_map/ppermute | solution.py:12
  276.6 12.5 %collective-permute-start.6 = (bf16[256,512]{1,0:T(8,128)(2,1)}, bf16[256,512]{1,0:T(8,128)(2,1)}, u32[]{:S(2)}, u32[]{:S(2)}) collective-permute-start(bf16[256,512]{1,0:T(8,128)(2,1)} %convolution_convert_fusion.8), channel_id=1, source_target_pairs={{0,16},{1,17},{2,18},{3,19},{4,20},{5,21},{6,22},{7,23},{8,24},{9,... | collective-permute-start | bytes 786440 | tf_op jit(solution)/shard_map/ppermute | solution.py:12
  283.8 9.2 %copy-start.9 = (pred[256,512]{1,0:T(8,128)(4,1)S(1)}, pred[256,512]{1,0:T(8,128)(4,1)}, u32[]{:S(2)}) copy-start(pred[256,512]{1,0:T(8,128)(4,1)} %fusion.87) | copy-start | bytes 393220
  300.8 2.5 copy-start.12
  302.3 0.8 copy-start.6
where the time goes:
time: 333 us; the launch traced here: 327 us
  matrix products  114 us (34%)
  waiting for transfers between devices  107 us (32%)
  local copies, waits for them, and re-layouts  44.2 us (13%)
  other arithmetic  39 us (12%)
  starting transfers between devices  22.4 us (7%)
    ppermute x9, waiting for transfers between devices, partner(): return lax.ppermute(value, axis, pairs)  107 us
    sub x3, matrix products, attend(): weights = jnp.exp(scores - row_top)  45.8 us
    dot_general x3, matrix products, attend(): jnp.einsum('hqk,khd->qhd', weights, value_heads, preferred_element_type=j...  36.4 us
    dot_general x13, matrix products, product(): return jnp.dot(values, weight, preferred_element_type=jnp.float32)  32.3 us
    ppermute x9, starting transfers between devices, partner(): return lax.ppermute(value, axis, pairs)  22.4 us
    concatenate x3, local copies, waits for them, and re-layouts, per_device(): joined_keys = jnp.concatenate([key_rows, far_keys], axis=0)  7.38 us
    concatenate x3, local copies, waits for them, and re-layouts, per_device(): joined_values = jnp.concatenate([value_rows, far_values], axis=0)  7.36 us
    reduce_sum x2, other arithmetic, per_device(): jnp.mean(current.reshape(rows_now // 2, 2, model_width).astype(jnp.float3...  7.34 us
  transfers between devices with their start and end apart: 9, of which 7 were waited for; matrix products, arithmetic and copies ran while one was open for 14% of the time, Pallas kernels for 0%

commit v1 on v0

v1 whole, which is shorter than its diff:
```python
import functools
import jax
import jax.numpy as jnp
from jax import lax
from jax.experimental import pallas as pl
from jax.experimental.pallas import tpu as pltpu
from jax.sharding import PartitionSpec as P

D = 512
HEAD = 64
HEADS = 8
VROWS = 80
LIMIT2 = 90.0**2
QSCALE = HEAD ** (-0.5) * 1.4426950408889634
NT = (((1,), (1,)), ((), ()))
TN = (((0,), (0,)), ((), ()))
BF = jnp.bfloat16
F32 = jnp.float32
VMEM = pl.BlockSpec(memory_space=pltpu.VMEM)
ANY = pl.BlockSpec(memory_space=pl.ANY)


def dotf(a, b, dims=(((1,), (0,)), ((), ()))):
    return lax.dot_general(a, b, dims, preferred_element_type=F32)


def norm_rows(values, gain):
    wide = values.astype(F32)
    centre = jnp.mean(wide, axis=-1, keepdims=True)
    wide = wide - centre
    spread = jnp.mean(jnp.square(wide), axis=-1, keepdims=True)
    return (wide * lax.rsqrt(spread + 1e-05) * gain).astype(BF)


def to_column(row):
    eye = lax.broadcasted_iota(jnp.int32, (128, 128), 0) == lax.broadcasted_iota(
        jnp.int32, (128, 128), 1
    )
    parts = []
    for start in range(0, row.shape[1], 128):
        block = jnp.where(eye, row[:, start : start + 128], 0.0)
        parts.append(jnp.sum(block, axis=1, keepdims=True))
    return jnp.concatenate(parts, axis=0)


def head_select():
    lane = lax.broadcasted_iota(jnp.int32, (16, D), 1)
    head = lax.broadcasted_iota(jnp.int32, (16, D), 0)
    return jnp.where(lane // HEAD == head, 1.0, 0.0).astype(BF)


def head_peak(rows):
    wide = rows.astype(F32)
    sums = dotf(head_select(), (wide * wide).astype(BF), NT)
    return jnp.broadcast_to(jnp.max(sums, axis=1, keepdims=True), (16, 128))


def split_keys(keys, km_ref):
    low = lax.broadcasted_iota(jnp.int32, (1, 128), 1) < HEAD
    for pair in range(HEADS // 2):
        part = keys[:, pair * 128 : (pair + 1) * 128]
        km_ref[2 * pair] = jnp.where(low, part, jnp.zeros_like(part))
        km_ref[2 * pair + 1] = jnp.where(low, jnp.zeros_like(part), part)


def split_values(values_t, fill_row, va_ref):
    width = values_t.shape[1]
    first = lax.broadcasted_iota(jnp.int32, (16, width), 0) == 0
    ones = jnp.where(first, fill_row, 0.0).astype(BF)
    for head in range(HEADS):
        part = values_t[head * HEAD : (head + 1) * HEAD].astype(F32)
        va_ref[head, :HEAD, :] = (part * fill_row).astype(BF)
        va_ref[head, HEAD:, :] = ones


def attend(q_ref, km_ref, va_ref, o_ref, add_ref):
    blocks = km_ref.shape[1] // 256

    def body(pair, carry):
        queries = q_ref[:, pl.ds(pl.multiple_of(pair * 128, 128), 128)]
        waiting = []

        def finish(head, block, scores, total):
            weights = jnp.exp2(scores).astype(BF)
            values = va_ref[pair * 2 + head, :, block * 256 : (block + 1) * 256]
            part = dotf(values, weights)
            return part if total is None else total + part

        totals = [None, None]

        def drain():
            head, block, scores = waiting.pop(0)
            totals[head] = finish(head, block, scores, totals[head])
            if block == blocks - 1:
                out = totals[head]
                if add_ref is not None:
                    out = out + add_ref[pair * 2 + head]
                o_ref[pair * 2 + head] = out

        for head in range(2):
            for block in range(blocks):
                keys = km_ref[pair * 2 + head, block * 256 : (block + 1) * 256, :]
                waiting.append((head, block, dotf(keys, queries, NT)))
                if len(waiting) > 1:
                    drain()
        while waiting:
            drain()
        return carry

    lax.fori_loop(0, HEADS // 2, body, 0)


def project_kv(normed, kw_ref, vw_ref):
    keys = dotf(normed, kw_ref[...]).astype(BF)
    values_t = dotf(vw_ref[...], normed, (((0,), (1,)), ((), ()))).astype(BF)
    return keys, values_t


def local_kernel(level, x_ref, fill_ref, gain_ref, qw_ref, kw_ref, vw_ref,
                 q_ref, k_ref, vt_ref, o_ref, qp_ref, kp_ref, km_ref, va_ref):
    rows = k_ref.shape[0]
    fill = fill_ref[...].astype(F32)
    normed = norm_rows(x_ref[:rows, :], gain_ref[...])
    if level == 0:
        normed = normed * to_column(fill).astype(BF)
    queries = (dotf(normed, qw_ref[...]) * QSCALE).astype(BF)
    q_ref[...] = queries
    keys, values_t = project_kv(normed, kw_ref, vw_ref)
    k_ref[...] = keys
    vt_ref[...] = values_t
    qp_ref[...] = head_peak(queries)
    kp_ref[...] = head_peak(keys)
    split_keys(keys, km_ref)
    split_values(values_t, fill, va_ref)
    attend(q_ref, km_ref, va_ref, o_ref, None)
    if level == 0:
        for head in range(HEADS):
            o_ref[head, HEAD : HEAD + 1, :] += 1.0 - fill
    else:
        prod = queries.astype(F32) * keys.astype(F32)
        high = prod.astype(BF)
        rest = (prod - high.astype(F32)).astype(BF)
        select = head_select()
        own = jnp.exp2(dotf(select, high, NT) + dotf(select, rest, NT))
        own = own * (1.0 - fill)
        for head in range(HEADS):
            weight = own[head : head + 1]
            part = values_t[head * HEAD : (head + 1) * HEAD].astype(F32)
            o_ref[head, :HEAD, :] += part * weight
            o_ref[head, HEAD : HEAD + 1, :] += weight


def remote_kernel(x_ref, fill_ref, gain_ref, kw_ref, vw_ref, q_ref, kp_in, o_in,
                  o_ref, kp_ref, km_ref, va_ref):
    rows = km_ref.shape[1]
    normed = norm_rows(x_ref[:rows, :], gain_ref[...])
    keys, values_t = project_kv(normed, kw_ref, vw_ref)
    kp_ref[...] = jnp.maximum(kp_in[...], head_peak(keys))
    split_keys(keys, km_ref)
    split_values(values_t, fill_ref[...].astype(F32), va_ref)
    attend(q_ref, km_ref, va_ref, o_ref, o_in)


def exact_attend(level, q_ref, fills, chunk_refs, chunk_rows, gain_ref, kw_ref, vw_ref,
                 k_loc, vt_loc, att_ref, xbuf, kf, vf):
    rows = q_ref.shape[0]
    pltpu.sync_copy(k_loc, kf.at[pl.ds(0, rows), :])
    pltpu.sync_copy(vt_loc, vf.at[:, pl.ds(0, rows)])
    at = rows
    for ref, count in zip(chunk_refs, chunk_rows):
        pltpu.sync_copy(ref.at[pl.ds(0, count), :], xbuf.at[pl.ds(0, count), :])
        normed = norm_rows(xbuf[:count, :], gain_ref[...])
        keys, values_t = project_kv(normed, kw_ref, vw_ref)
        kf[at : at + count, :] = keys
        vf[:, at : at + count] = values_t
        at += count
    total = 2 * rows
    low = lax.broadcasted_iota(jnp.int32, (1, 128), 1) < HEAD
    fill8 = jnp.broadcast_to(jnp.concatenate(fills, axis=1), (8, total)).astype(BF)
    width = 128

    def body(step, carry):
        pair = step // (rows // width)
        start = pl.multiple_of(step % (rows // width) * width, width)
        lanes = pl.ds(pl.multiple_of(pair * 128, 128), 128)
        queries = q_ref[pl.ds(start, width), lanes]
        keys = kf[:, lanes]
        mask = dotf(fill8, jnp.ones((8, width), BF), TN) > 0.5
        own = lax.broadcasted_iota(jnp.int32, (total, width), 0) == (
            lax.broadcasted_iota(jnp.int32, (total, width), 1) + start
        )
        allowed = mask | own
        for head in range(2):
            part = jnp.where(low if head == 0 else ~low, keys, jnp.zeros_like(keys))
            scores = jnp.where(allowed, dotf(part, queries, NT), -1e30)
            weights = jnp.exp2(scores - jnp.max(scores, axis=0, keepdims=True))
            weights = weights / jnp.sum(weights, axis=0, keepdims=True)
            first = pl.multiple_of(pair * 128 + head * HEAD, HEAD)
            values = vf[pl.ds(first, HEAD), :]
            att_ref[pl.ds(first, HEAD), pl.ds(start, width)] = dotf(
                values, weights.astype(BF)
            ).astype(BF)
        return carry

    lax.fori_loop(0, HEADS // 2 * (rows // width), body, 0)


def finish_attention(level, refs, chunk_refs, chunk_rows, fill, fills_far):
    (gain_ref, kw_ref, vw_ref, q_ref, qp_ref, kp_ref, o_in, k_loc, vt_loc,
     att_ref, km_ref, va_ref, o_scr, xbuf, kf, vf, last_ref) = refs
    rows = km_ref.shape[1]
    normed = norm_rows(last_ref[:rows, :], gain_ref[...])
    keys, values_t = project_kv(normed, kw_ref, vw_ref)
    peak = jnp.maximum(kp_ref[...], head_peak(keys)) * qp_ref[...]
    split_keys(keys, km_ref)
    split_values(values_t, fills_far[-1], va_ref)
    attend(q_ref, km_ref, va_ref, o_scr, o_in)
    for head in range(HEADS):
        scale = 1.0 / o_scr[head, HEAD : HEAD + 1, :]
        att_ref[head * HEAD : (head + 1) * HEAD, :] = (o_scr[head, :HEAD, :] * scale).astype(BF)
    inside = jnp.max(peak) <= LIMIT2

    @pl.when(jnp.logical_not(inside))
    def _():
        exact_attend(level, q_ref, [fill] + fills_far, chunk_refs, chunk_rows, gain_ref,
                     kw_ref, vw_ref, k_loc, vt_loc, att_ref, xbuf, kf, vf)


def finish0_kernel(counts, *refs):
    n = len(counts)
    chunks, rest = refs[:n], refs[n:]
    (last_ref, fill_ref, far_ref, gain_ref, kw_ref, vw_ref, ow_ref, q_ref, qp_ref, kp_ref, o_in,
     k_loc, vt_loc, points_ref, tree_ref,
     y_ref, xa_ref, xb_ref, f_ref, att_ref, km_ref, va_ref, o_scr, xbuf, kf, vf) = rest
    fill = fill_ref[...].astype(F32)
    far = far_ref[...].astype(F32)
    fills_far, at = [], 0
    for count in counts:
        fills_far.append(far[:, at : at + count])
        at += count
    finish_attention(0, (gain_ref, kw_ref, vw_ref, q_ref, qp_ref, kp_ref, o_in, k_loc, vt_loc,
                         att_ref, km_ref, va_ref, o_scr, xbuf, kf, vf, last_ref),
                     chunks, counts, fill, fills_far)
    x0 = points_ref[...].astype(F32) * to_column(fill)
    y = (x0 + dotf(att_ref[...], ow_ref[...], TN)).astype(BF)
    y_ref[...] = y
    lanes = lax.broadcasted_iota(jnp.int32, (256, 1024), 1)
    f8 = jnp.broadcast_to(fill, (8, 1024)).astype(BF)
    for half, out in ((0, xa_ref), (1, xb_ref)):
        picked = (lanes == tree_ref[:, 2 * half : 2 * half + 1]) | (
            lanes == tree_ref[:, 2 * half + 1 : 2 * half + 2]
        )
        pool = jnp.where(picked, 0.5, 0.0).astype(BF)
        out[:256, :] = dotf(pool, y).astype(BF)
        f_half = jnp.where(dotf(f8, pool, NT)[:1] > 0.25, 1.0, 0.0)
        f_ref[:, half * 256 : (half + 1) * 256] = f_half


def finish1_kernel(counts, *refs):
    n = len(counts)
    chunks, rest = refs[:n], refs[n:]
    (last_ref, fill_ref, far_ref, gain_ref, kw_ref, vw_ref, ow_ref, q_ref, qp_ref, kp_ref, o_in,
     k_loc, vt_loc, x_ref,
     y_ref, x2_ref, f_ref, att_ref, km_ref, va_ref, o_scr, xbuf, kf, vf) = rest
    fill = fill_ref[...].astype(F32)
    far = far_ref[...].astype(F32)
    fills_far, at = [], 0
    for count in counts:
        fills_far.append(far[:, at : at + count])
        at += count
    finish_attention(1, (gain_ref, kw_ref, vw_ref, q_ref, qp_ref, kp_ref, o_in, k_loc, vt_loc,
                         att_ref, km_ref, va_ref, o_scr, xbuf, kf, vf, last_ref),
                     chunks, counts, fill, fills_far)
    y = (x_ref[...].astype(F32) + dotf(att_ref[...], ow_ref[...], TN)).astype(BF)
    y_ref[...] = y
    wide = y.astype(F32)
    x2_ref[:256, :] = ((wide[:256] + wide[256:]) * 0.5).astype(BF)
    f_ref[...] = jnp.maximum(fill[:, :256], fill[:, 256:])


def finish2_kernel(counts, *refs):
    n = len(counts)
    chunks, rest = refs[:n], refs[n:]
    (last_ref, fill_ref, far_ref, gain_ref, kw_ref, vw_ref, ow_ref, q_ref, qp_ref, kp_ref, o_in,
     k_loc, vt_loc, x_ref, gm_ref, hw_ref, pw_ref, y1_ref, y0_ref, tree_ref,
     field_ref, att_ref, km_ref, va_ref, o_scr, xbuf, kf, vf) = rest
    fill = fill_ref[...].astype(F32)
    far = far_ref[...].astype(F32)
    finish_attention(2, (gain_ref, kw_ref, vw_ref, q_ref, qp_ref, kp_ref, o_in, k_loc, vt_loc,
                         att_ref, km_ref, va_ref, o_scr, xbuf, kf, vf, last_ref),
                     chunks, counts, fill, [far])
    y2 = (x_ref[:256, :].astype(F32) + dotf(att_ref[...], ow_ref[...], TN)).astype(BF)
    normed = norm_rows(y2, gm_ref[...])
    hidden = jax.nn.gelu(dotf(normed, hw_ref[...]), approximate=True).astype(BF)
    top = (y2.astype(F32) + dotf(hidden, pw_ref[...])).astype(BF).astype(F32)
    up = [(y1_ref[half * 256 : (half + 1) * 256, :].astype(F32) + top).astype(BF)
          for half in range(2)]
    rows = lax.broadcasted_iota(jnp.int32, (1024, 256), 0)
    total = y0_ref[...].astype(F32)
    for half in range(2):
        picked = (rows == tree_ref[2 * half : 2 * half + 1, :]) | (
            rows == tree_ref[2 * half + 1 : 2 * half + 2, :]
        )
        total = total + dotf(jnp.where(picked, 1.0, 0.0).astype(BF), up[half])
    field_ref[...] = total.astype(BF)


def call(kernel, outs, args, in_any=(), scratch=(), flops=0):
    nbytes = sum(a.size * a.dtype.itemsize for a in args) + sum(
        a.size * a.dtype.itemsize for a in outs)
    return pl.pallas_call(
        kernel,
        out_shape=outs,
        in_specs=[ANY if i in in_any else VMEM for i in range(len(args))],
        out_specs=[VMEM] * len(outs),
        scratch_shapes=list(scratch),
        compiler_params=pltpu.CompilerParams(vmem_limit_bytes=56 * 2**20),
        cost_estimate=pl.CostEstimate(flops=flops, bytes_accessed=nbytes, transcendentals=0),
    )(*args)


def shape(*dims, dtype=BF):
    return jax.ShapeDtypeStruct(dims, dtype)


def local_part(level, x, fill, gain, qw, kw, vw, rows):
    return call(
        functools.partial(local_kernel, level),
        [shape(rows, D), shape(rows, D), shape(D, rows), shape(HEADS, VROWS, rows, dtype=F32),
         shape(16, 128, dtype=F32), shape(16, 128, dtype=F32)],
        [x, fill, gain, qw, kw, vw],
        scratch=[pltpu.VMEM((HEADS, rows, 128), BF), pltpu.VMEM((HEADS, VROWS, rows), BF)],
        flops=8 * rows * rows * 512 * 2,
    )


def remote_part(x, fill, gain, kw, vw, q, kp, o, count):
    rows = q.shape[0]
    return call(
        remote_kernel,
        [shape(HEADS, VROWS, rows, dtype=F32), shape(16, 128, dtype=F32)],
        [x, fill, gain, kw, vw, q, kp, o],
        scratch=[pltpu.VMEM((HEADS, count, 128), BF), pltpu.VMEM((HEADS, VROWS, count), BF)],
        flops=8 * rows * count * 512 * 2,
    )


def finish_part(kernel, counts, chunks, args, outs, rows):
    n = len(counts)
    inputs = list(chunks) + [chunks[-1]] + args
    return call(
        functools.partial(kernel, counts),
        outs,
        inputs,
        in_any=set(range(n)) | {n + 11, n + 12},
        scratch=[
            pltpu.VMEM((D, rows), BF),
            pltpu.VMEM((HEADS, counts[-1], 128), BF),
            pltpu.VMEM((HEADS, VROWS, counts[-1]), BF),
            pltpu.VMEM((HEADS, VROWS, rows), F32),
            pltpu.VMEM((max(counts), D), BF),
            pltpu.VMEM((2 * rows, D), BF),
            pltpu.VMEM((D, 2 * rows), BF),
        ],
        flops=8 * rows * counts[-1] * 512 * 2 + 4 * rows * D * D,
    )


def per_device(points, tree_order, present, gain_attn, query_weight, key_weight, value_weight,
               out_weight, gain_mlp, hidden_weight, proj_weight):
    size = lax.axis_size("leaf")

    def trade(value, bit):
        return lax.ppermute(value, "leaf", [(s, s ^ (1 << bit)) for s in range(size)])

    base = size.bit_length() - 1 - 3
    fill0 = present.reshape(1, 1024)
    far_fill = trade(fill0, base)
    counts0 = (256, 256, 256, 256)
    chunks, at = [], 0
    for i, count in enumerate(counts0):
        part = points[at : at + count]
        if i >= 2:
            part, _ = lax.optimization_barrier((part, chunks[i - 2]))
        chunks.append(trade(part, base))
        at += count
    tree4 = tree_order.reshape(256, 4)
    tree_rows = tree4.T

    def gain(level):
        return gain_attn[level].reshape(1, D)

    q, k, vt, o, qp, kp = local_part(0, points, fill0, gain(0), query_weight[0], key_weight[0],
                                     value_weight[0], 1024)
    at = 0
    for chunk, count in zip(chunks[:-1], counts0[:-1]):
        o, kp = remote_part(chunk, far_fill[:, at : at + count], gain(0), key_weight[0],
                            value_weight[0], q, kp, o, count)
        at += count
    y0, xa, xb, f1 = finish_part(
        finish0_kernel, counts0, chunks,
        [fill0, far_fill, gain(0), key_weight[0], value_weight[0], out_weight[0], q, qp, kp, o, k,
         vt, points, tree4],
        [shape(1024, D), shape(256, D), shape(256, D), shape(1, 512, dtype=F32)], 1024)
    far_f1 = trade(f1, base + 1)
    far_a = trade(xa, base + 1)
    far_b = trade(xb, base + 1)
    x1 = jnp.concatenate([xa, xb], axis=0)
    q, k, vt, o, qp, kp = local_part(1, x1, f1, gain(1), query_weight[1], key_weight[1],
                                     value_weight[1], 512)
    o, kp = remote_part(far_a, far_f1[:, :256], gain(1), key_weight[1], value_weight[1], q, kp, o,
                        256)
    y1, x2, f2 = finish_part(
        finish1_kernel, (256, 256), [far_a, far_b],
        [f1, far_f1, gain(1), key_weight[1], value_weight[1], out_weight[1], q, qp, kp, o, k, vt,
         x1],
        [shape(512, D), shape(256, D), shape(1, 256, dtype=F32)], 512)
    far_f2 = trade(f2, base + 2)
    far_x2 = trade(x2, base + 2)
    q, k, vt, o, qp, kp = local_part(2, x2, f2, gain(2), query_weight[2], key_weight[2],
                                     value_weight[2], 256)
    (field,) = finish_part(
        finish2_kernel, (256,), [far_x2],
        [f2, far_f2, gain(2), key_weight[2], value_weight[2], out_weight[2], q, qp, kp, o, k, vt,
         x2, gain_mlp.reshape(1, D), hidden_weight, proj_weight, y1, y0, tree_rows],
        [shape(1024, D)], 256)
    return field


def solution(mesh):
    placed = (
        P(("cloud", "leaf"), None),
        P(("cloud", "leaf")),
        P(("cloud", "leaf")),
        P(), P(), P(), P(), P(), P(), P(), P(),
    )
    return jax.shard_map(
        per_device,
        mesh=mesh,
        in_specs=placed,
        out_specs=P(("cloud", "leaf"), None),
        check_vma=False,
    )
```

time: 333 us -> 234 us (0.70); the launches traced: 327 us -> 233 us
  Pallas kernels: 0 us -> 188 us
  matrix products: 114 us -> 0 us
  waiting for transfers between devices: 107 us -> 5.07 us
  other arithmetic: 39 us -> 0 us
  local copies, waits for them, and re-layouts: 44.2 us -> 16.2 us
    pallas_call x0 -> x10, Pallas kernels: none -> 188 us  [call(): pl.pallas_call(kernel, out_shape=outs, in_specs=[ANY if i in in_any else...]
    ppermute x9 -> x10, waiting for transfers between devices: 107 us -> 5.07 us  [trade(): return lax.ppermute(value, 'leaf', [(s, s ^ 1 << bit) for s in range(size)])]
    dot_general x16 -> x0, matrix products: 68.7 us -> none  [the longest x3 36.4 us: attend(): jnp.einsum('hqk,khd->qhd', weights, value_heads, preferred_element_type=j...]
    sub x3 -> x0, matrix products: 45.8 us -> none  [attend(): weights = jnp.exp(scores - row_top)]
    convert_element_type x6 -> x0, local copies, waits for them, and re-layouts: 13.9 us -> none  [the longest x2 6.64 us: per_device(): spread_rows.astype(jnp.float32)]
    concatenate x6 -> x1, local copies, waits for them, and re-layouts: 14.7 us -> 1 us  [per_device(): x1 = jnp.concatenate([xa, xb], axis=0)]
    reduce_sum x9 -> x0, other arithmetic: 13 us -> none  [the longest x2 7.34 us: per_device(): jnp.mean(current.reshape(rows_now // 2, 2, model_width).astype(jnp.float3...]
    concatenate x6 -> x0, other arithmetic: 11.1 us -> none  [the longest x3 6.15 us: per_device(): joined_values = jnp.concatenate([value_rows, far_values], axis=0)]
  transfers between devices with their start and end apart: 9 -> 10, of which waited for: 7 -> 2; matrix products, arithmetic and copies ran while one was open for 14% -> 4% of each run, Pallas kernels for 0% -> 24%
where the time goes in v1:
time: 234 us; the launch traced here: 233 us
  Pallas kernels  188 us (80%)
  starting transfers between devices  23.3 us (10%)
  local copies, waits for them, and re-layouts  16.2 us (7%)
  waiting for transfers between devices  5.07 us (2%)
    pallas_call x10, Pallas kernels, call(): pl.pallas_call(kernel, out_shape=outs, in_specs=[ANY if i in in_any else...  188 us
    ppermute x10, starting transfers between devices, trade(): return lax.ppermute(value, 'leaf', [(s, s ^ 1 << bit) for s in range(size)])  23.3 us
    unnamed x39, local copies, waits for them, and re-layouts  6.52 us
    ppermute x10, waiting for transfers between devices, trade(): return lax.ppermute(value, 'leaf', [(s, s ^ 1 << bit) for s in range(size)])  5.07 us
  transfers between devices with their start and end apart: 10, of which 2 were waited for; matrix products, arithmetic and copies ran while one was open for 4% of the time, Pallas kernels for 24%

profile of v1, /device:TPU:18, one launch (start us, length us, event | category | flops | bytes accessed | tf_op | source)
XLA Modules:
  0.0 232.8 jit_solution(780251331191395726)
XLA Ops:
  0.0 0.0 copy-start.18
  0.0 1.4 fusion
  1.4 3.4 %collective-permute-start = (bf16[256,512]{1,0:T(8,128)(2,1)S(1)}, bf16[256,512]{1,0:T(8,128)(2,1)S(1)}, u32[]{:S(2)}, u32[]{:S(2)}) collective-permute-start(bf16[256,512]{1,0:T(8,128)(2,1)S(1)} %get-tuple-element.90), channel_id=1, source_target_pairs={{0,4},{1,5},{2,6},{3,7},{4,0},{5,1},{6,2},{7,3},{8,12},{9,13},{10,... | collective-permute-start | bytes 786440 | tf_op jit(solution)/shard_map/ppermute | solution.py:374
  4.7 0.0 copy-done.18
  4.8 0.1 collective-permute-start.4
  4.9 2.8 %collective-permute-start.1 = (bf16[256,512]{1,0:T(8,128)(2,1)S(1)}, bf16[256,512]{1,0:T(8,128)(2,1)S(1)}, u32[]{:S(2)}, u32[]{:S(2)}) collective-permute-start(bf16[256,512]{1,0:T(8,128)(2,1)S(1)} %get-tuple-element.89), channel_id=1, source_target_pairs={{0,4},{1,5},{2,6},{3,7},{4,0},{5,1},{6,2},{7,3},{8,12},{9,13},{10,... | collective-permute-start | bytes 786440 | tf_op jit(solution)/shard_map/ppermute | solution.py:374
  7.7 0.0 copy-done.7
  7.7 0.6 fusion.1
  8.3 0.0 copy-done
  8.3 1.2 slice_bitcast_fusion
  9.5 0.8 copy-done.2
  10.2 0.5 copy-done.3
  10.7 1.7 slice_bitcast_fusion.2
  12.5 14.6 %shard_map.109 = (bf16[1024,512]{1,0:T(8,128)(2,1)}, bf16[1024,512]{1,0:T(8,128)(2,1)}, bf16[512,1024]{1,0:T(8,128)(2,1)}, f32[8,80,1024]{2,1,0:T(8,128)}, f32[16,128]{1,0:T(8,128)}, /*index=5*/f32[16,128]{1,0:T(8,128)}) custom-call(bf16[1024,512]{1,0:T(8,128)(2,1)} %refs_17_.2, s32[1,1024]{1,0:T(1,128)} %bitcast.29, ...), custom_call_target="tpu_custom_call" | custom-call | flops 8589934592 | bytes 8411136 | tf_op jit(solution)/shard_map/pallas_call | solution.py:311
  27.0 0.0 copy-done.1
  27.0 1.2 slice_bitcast_fusion.1
  28.3 0.0 copy-done.8
  28.3 0.8 reshape.10.refs_18_
  29.0 0.0 collective-permute-done.4.refs_6_
  29.0 0.6 fusion.2
  29.6 0.0 collective-permute-done.x_ref.refs_0_
  29.6 0.1 collective-permute-start.2
  29.8 0.0 collective-permute-done.1.x_ref.refs_1_
  29.8 2.8 %collective-permute-start.3 = (bf16[256,512]{1,0:T(8,128)(2,1)S(1)}, bf16[256,512]{1,0:T(8,128)(2,1)S(1)}, u32[]{:S(2)}, u32[]{:S(2)}) collective-permute-start(bf16[256,512]{1,0:T(8,128)(2,1)S(1)} %get-tuple-element.41), channel_id=1, source_target_pairs={{0,4},{1,5},{2,6},{3,7},{4,0},{5,1},{6,2},{7,3},{8,12},{9,13},{10,... | collective-permute-start | bytes 786440 | tf_op jit(solution)/shard_map/ppermute | solution.py:374
  32.6 0.0 copy-done.12
  32.6 7.2 %shard_map.110 = (f32[8,80,1024]{2,1,0:T(8,128)}, f32[16,128]{1,0:T(8,128)}) custom-call(bf16[256,512]{1,0:T(8,128)(2,1)} %copy-done.12, s32[1,256]{1,0:T(1,128)} %get-tuple-element.94.fill_ref, f32[1,512]{1,0:T(1,128)} %get-tuple-element.92.gain_ref.refs_7_, bf16[512,512]{1,0:T(8,128)(2,1)} %get-tuple-element.98.kw_ref.refs_8_, ...), custom_call_target="tpu_custom_call" | custom-call | flops 2147483648 | bytes 7621632 | tf_op jit(solution)/shard_map/pallas_call | solution.py:311
  39.8 0.0 copy-done.9
  39.8 0.0 copy-done.13
  39.8 7.3 %shard_map.111 = (f32[8,80,1024]{2,1,0:T(8,128)}, f32[16,128]{1,0:T(8,128)}) custom-call(bf16[256,512]{1,0:T(8,128)(2,1)} %copy-done.13, s32[1,256]{1,0:T(1,128)} %get-tuple-element.95.fill_ref, f32[1,512]{1,0:T(1,128)} %get-tuple-element.92.gain_ref.refs_7_, bf16[512,512]{1,0:T(8,128)(2,1)} %get-tuple-element.98.kw_ref.refs_8_, ...), custom_call_target="tpu_custom_call" | custom-call | flops 2147483648 | bytes 7621632 | tf_op jit(solution)/shard_map/pallas_call | solution.py:311
  47.1 3.4 %collective-permute-done.2.x_ref.refs_2_ = bf16[256,512]{1,0:T(8,128)(2,1)S(1)} collective-permute-done((bf16[256,512]{1,0:T(8,128)(2,1)S(1)}, bf16[256,512]{1,0:T(8,128)(2,1)S(1)}, u32[]{:S(2)}, u32[]{:S(2)}) %collective-permute-start.2) | collective-permute-done | bytes 262176 | tf_op jit(solution)/shard_map/ppermute | solution.py:374
  50.5 0.7 copy-done.14
  51.2 7.2 %shard_map.112 = (f32[8,80,1024]{2,1,0:T(8,128)}, f32[16,128]{1,0:T(8,128)}) custom-call(bf16[256,512]{1,0:T(8,128)(2,1)} %copy-done.14, s32[1,256]{1,0:T(1,128)} %get-tuple-element.96.fill_ref, f32[1,512]{1,0:T(1,128)} %get-tuple-element.92.gain_ref.refs_7_, bf16[512,512]{1,0:T(8,128)(2,1)} %get-tuple-element.98.kw_ref.refs_8_, ...), custom_call_target="tpu_custom_call" | custom-call | flops 2147483648 | bytes 7621632 | tf_op jit(solution)/shard_map/pallas_call | solution.py:311
  58.4 0.0 collective-permute-done.3.refs_3_.refs_4_
  58.4 0.7 copy-done.15
  59.1 83.8 %shard_map.113 = (bf16[1024,512]{1,0:T(8,128)(2,1)}, bf16[256,512]{1,0:T(8,128)(2,1)}, bf16[256,512]{1,0:T(8,128)(2,1)}, f32[1,512]{1,0:T(1,128)}) custom-call(bf16[256,512]{1,0:T(8,128)(2,1)} %copy-done.12, bf16[256,512]{1,0:T(8,128)(2,1)} %copy-done.13, bf16[256,512]{1,0:T(8,128)(2,1)} %copy-done.14, bf16[256,512]{1,0:T(8,128)(2,1)} %copy-done.15, ...), custom_call_target="tpu_custom_call" | custom-call | flops 3221225472 | bytes 11304960 | tf_op jit(solution)/shard_map/pallas_call | solution.py:311
  143.0 1.0 constant_dynamic-update-slice_fusion.1
  143.9 4.6 %collective-permute-start.5 = (bf16[256,512]{1,0:T(8,128)(2,1)}, bf16[256,512]{1,0:T(8,128)(2,1)S(1)}, u32[]{:S(2)}, u32[]{:S(2)}) collective-permute-start(bf16[256,512]{1,0:T(8,128)(2,1)} %get-tuple-element.54), channel_id=1, source_target_pairs={{0,8},{1,9},{2,10},{3,11},{4,12},{5,13},{6,14},{7,15},{8,0},{9,1},... | collective-permute-start | bytes 786440 | tf_op jit(solution)/shard_map/ppermute | solution.py:374
  148.5 1.4 collective-permute-start.7
  149.9 4.5 %collective-permute-start.6 = (bf16[256,512]{1,0:T(8,128)(2,1)}, bf16[256,512]{1,0:T(8,128)(2,1)S(1)}, u32[]{:S(2)}, u32[]{:S(2)}) collective-permute-start(bf16[256,512]{1,0:T(8,128)(2,1)} %get-tuple-element.55), channel_id=1, source_target_pairs={{0,8},{1,9},{2,10},{3,11},{4,12},{5,13},{6,14},{7,15},{8,0},{9,1},... | collective-permute-start | bytes 786440 | tf_op jit(solution)/shard_map/ppermute | solution.py:374
  154.5 1.0 constant_dynamic-update-slice_fusion.x_ref.refs_15_
  155.5 0.0 copy-start.6
  155.5 0.8 copy-done.6
  156.3 7.9 %shard_map.114 = (bf16[512,512]{1,0:T(8,128)(2,1)}, bf16[512,512]{1,0:T(8,128)(2,1)}, bf16[512,512]{1,0:T(8,128)(2,1)}, f32[8,80,512]{2,1,0:T(8,128)}, f32[16,128]{1,0:T(8,128)}, /*index=5*/f32[16,128]{1,0:T(8,128)}) custom-call(bf16[512,512]{1,0:T(8,128)(2,1)} %copy-done.6, f32[1,512]{1,0:T(1,128)} %get-tuple-element.56.fill_ref.refs_3_, ...), custom_call_target="tpu_custom_call" | custom-call | flops 2147483648 | bytes 5001216 | tf_op jit(solution)/shard_map/pallas_call | solution.py:311
  164.2 1.6 collective-permute-done.7.refs_4_
  165.8 0.6 slice.116.fill_ref
  166.4 0.0 collective-permute-done.5.x_ref.refs_0_
  166.4 0.7 copy-done.16
  167.1 5.7 %shard_map.115 = (f32[8,80,512]{2,1,0:T(8,128)}, f32[16,128]{1,0:T(8,128)}) custom-call(bf16[256,512]{1,0:T(8,128)(2,1)} %copy-done.16, f32[1,256]{1,0:T(1,128)} %slice.116.fill_ref, f32[1,512]{1,0:T(1,128)} %get-tuple-element.93.gain_ref.refs_5_, bf16[512,512]{1,0:T(8,128)(2,1)} %get-tuple-element.97.kw_ref.refs_6_, ...), custom_call_target="tpu_custom_call" | custom-call | flops 1073741824 | bytes 4475904 | tf_op jit(solution)/shard_map/pallas_call | solution.py:311
  172.8 0.0 copy-done.11
  172.8 0.0 collective-permute-done.6.refs_1_.refs_2_
  172.8 0.0 copy-start.17
  172.8 0.7 copy-done.17
  173.5 31.4 %shard_map.116 = (bf16[512,512]{1,0:T(8,128)(2,1)}, bf16[256,512]{1,0:T(8,128)(2,1)}, f32[1,256]{1,0:T(1,128)}) custom-call(bf16[256,512]{1,0:T(8,128)(2,1)} %copy-done.16, bf16[256,512]{1,0:T(8,128)(2,1)} %copy-done.17, bf16[256,512]{1,0:T(8,128)(2,1)} %copy-done.17, f32[1,512]{1,0:T(1,128)} %get-tuple-element.56.fill_ref.refs_3_, f32[1,512]{1,0:T(1,128)} %copy-done.11, ...), custom_call_target="tpu_custom_call" | custom-call | flops 1610612736 | bytes 6577152 | tf_op jit(solution)/shard_map/pallas_call | solution.py:311
  204.9 0.3 collective-permute-start.8
  205.2 0.0 copy-done.5
  205.2 0.7 copy.13
  205.9 3.2 %collective-permute-start.9 = (f32[1,256]{1,0:T(1,128)}, f32[1,256]{1,0:T(1,128)S(1)}, u32[]{:S(2)}, u32[]{:S(2)}) collective-permute-start(f32[1,256]{1,0:T(1,128)} %get-tuple-element.66.fill_ref.refs_2_), channel_id=1, source_target_pairs={{0,16},{1,17},{2,18},{3,19},{4,20},{5,21},{6,22},{7,23},{8,24},{9,... | collective-permute-start | bytes 3080 | tf_op jit(solution)/shard_map/ppermute | solution.py:374
  209.1 5.1 %shard_map.117 = (bf16[256,512]{1,0:T(8,128)(2,1)}, bf16[256,512]{1,0:T(8,128)(2,1)}, bf16[512,256]{1,0:T(8,128)(2,1)}, f32[8,80,256]{2,1,0:T(8,128)}, f32[16,128]{1,0:T(8,128)}, /*index=5*/f32[16,128]{1,0:T(8,128)}) custom-call(bf16[256,512]{1,0:T(8,128)(2,1)} %get-tuple-element.65.x_ref.refs_14_, f32[1,256]{1,0:T(1,128)} %get-tuple-element.66.fill_ref.refs_2_, ...), custom_call_target="tpu_custom_call" | custom-call | flops 536870912 | bytes 3296256 | tf_op jit(solution)/shard_map/pallas_call | solution.py:311
  214.2 0.0 collective-permute-done.9.refs_3_
  214.2 0.0 collective-permute-done.8.refs_0_.refs_1_
  214.2 0.0 copy-start.4
  214.3 0.5 copy-done.10
  214.8 0.2 copy-done.4
  215.0 17.8 %shard_map.118 = bf16[1024,512]{1,0:T(8,128)(2,1)} custom-call(bf16[256,512]{1,0:T(8,128)(2,1)} %copy-done.4, bf16[256,512]{1,0:T(8,128)(2,1)} %copy-done.4, f32[1,256]{1,0:T(1,128)} %get-tuple-element.66.fill_ref.refs_2_, f32[1,256]{1,0:T(1,128)} %copy-done.10, f32[1,512]{1,0:T(1,128)} %get-tuple-element.91.gain_ref.refs_4_, ...), custom_call_target="tpu_custom_call" | custom-call | flops 805306368 | bytes 10643456 | tf_op jit(solution)/shard_map/pallas_call | solution.py:311
  (15 shorter events, 0.0 us)
Async XLA Ops:
  0.0 4.8 %copy-start.18 = (s32[1024]{0:T(1024)S(1)}, s32[1024]{0:T(1024)}, u32[]{:S(2)}) copy-start(s32[1024]{0:T(1024)} %param.13) | copy-start | bytes 12292
  0.0 7.7 %copy-start.7 = (f32[3,512]{1,0:T(4,128)S(1)}, f32[3,512]{1,0:T(4,128)}, u32[]{:S(2)}) copy-start(f32[3,512]{1,0:T(4,128)} %param.14) | copy-start | bytes 18436
  0.0 8.3 %copy-start = (bf16[3,512,512]{2,1,0:T(8,128)(2,1)S(1)}, bf16[3,512,512]{2,1,0:T(8,128)(2,1)}, u32[]{:S(2)}) copy-start(bf16[3,512,512]{2,1,0:T(8,128)(2,1)} %param.15) | copy-start | bytes 4718596
  1.4 28.3 %collective-permute-start = (bf16[256,512]{1,0:T(8,128)(2,1)S(1)}, bf16[256,512]{1,0:T(8,128)(2,1)S(1)}, u32[]{:S(2)}, u32[]{:S(2)}) collective-permute-start(bf16[256,512]{1,0:T(8,128)(2,1)S(1)} %get-tuple-element.90), channel_id=1, source_target_pairs={{0,4},{1,5},{2,6},{3,7},{4,0},{5,1},{6,2},{7,3},{8,12},{9,13},{10,... | collective-permute-start | bytes 786440 | tf_op jit(solution)/shard_map/ppermute | solution.py:374
  4.8 24.3 %collective-permute-start.4 = (s32[1,1024]{1,0:T(1,128)S(1)}, s32[1,1024]{1,0:T(1,128)S(1)}, u32[]{:S(2)}, u32[]{:S(2)}) collective-permute-start(s32[1,1024]{1,0:T(1,128)S(1)} %bitcast.31), channel_id=1, source_target_pairs={{0,4},{1,5},{2,6},{3,7},{4,0},{5,1},{6,2},{7,3},{8,12},{9,13},{10,... | collective-permute-start | bytes 12296 | tf_op jit(solution)/shard_map/ppermute | solution.py:374
  4.9 24.9 %collective-permute-start.1 = (bf16[256,512]{1,0:T(8,128)(2,1)S(1)}, bf16[256,512]{1,0:T(8,128)(2,1)S(1)}, u32[]{:S(2)}, u32[]{:S(2)}) collective-permute-start(bf16[256,512]{1,0:T(8,128)(2,1)S(1)} %get-tuple-element.89), channel_id=1, source_target_pairs={{0,4},{1,5},{2,6},{3,7},{4,0},{5,1},{6,2},{7,3},{8,12},{9,13},{10,... | collective-permute-start | bytes 786440 | tf_op jit(solution)/shard_map/ppermute | solution.py:374
  8.3 2.0 copy-start.2
  8.3 2.4 %copy-start.3 = (bf16[3,512,512]{2,1,0:T(8,128)(2,1)S(1)}, bf16[3,512,512]{2,1,0:T(8,128)(2,1)}, u32[]{:S(2)}) copy-start(bf16[3,512,512]{2,1,0:T(8,128)(2,1)} %param.16) | copy-start | bytes 4718596
  12.5 14.6 %copy-start.1 = (bf16[3,512,512]{2,1,0:T(8,128)(2,1)S(1)}, bf16[3,512,512]{2,1,0:T(8,128)(2,1)}, u32[]{:S(2)}) copy-start(bf16[3,512,512]{2,1,0:T(8,128)(2,1)} %param.18) | copy-start | bytes 4718596
  27.0 1.2 copy-start.8
  29.0 10.8 %copy-start.9 = (s32[1,1024]{1,0:T(1,128)}, s32[1,1024]{1,0:T(1,128)S(1)}, u32[]{:S(2)}) copy-start(s32[1,1024]{1,0:T(1,128)S(1)} %collective-permute-done.4.refs_6_) | copy-start | bytes 12292
  29.6 2.9 %copy-start.12 = (bf16[256,512]{1,0:T(8,128)(2,1)}, bf16[256,512]{1,0:T(8,128)(2,1)S(1)}, u32[]{:S(2)}) copy-start(bf16[256,512]{1,0:T(8,128)(2,1)S(1)} %collective-permute-done.x_ref.refs_0_) | copy-start | bytes 786436
  29.6 20.8 %collective-permute-start.2 = (bf16[256,512]{1,0:T(8,128)(2,1)S(1)}, bf16[256,512]{1,0:T(8,128)(2,1)S(1)}, u32[]{:S(2)}, u32[]{:S(2)}) collective-permute-start(bf16[256,512]{1,0:T(8,128)(2,1)S(1)} %get-tuple-element.40), channel_id=1, source_target_pairs={{0,4},{1,5},{2,6},{3,7},{4,0},{5,1},{6,2},{7,3},{8,12},{9,13},{10,... | collective-permute-start | bytes 786440 | tf_op jit(solution)/shard_map/ppermute | solution.py:374
  29.8 10.1 %copy-start.13 = (bf16[256,512]{1,0:T(8,128)(2,1)}, bf16[256,512]{1,0:T(8,128)(2,1)S(1)}, u32[]{:S(2)}) copy-start(bf16[256,512]{1,0:T(8,128)(2,1)S(1)} %collective-permute-done.1.x_ref.refs_1_) | copy-start | bytes 786436
  29.8 28.6 %collective-permute-start.3 = (bf16[256,512]{1,0:T(8,128)(2,1)S(1)}, bf16[256,512]{1,0:T(8,128)(2,1)S(1)}, u32[]{:S(2)}, u32[]{:S(2)}) collective-permute-start(bf16[256,512]{1,0:T(8,128)(2,1)S(1)} %get-tuple-element.41), channel_id=1, source_target_pairs={{0,4},{1,5},{2,6},{3,7},{4,0},{5,1},{6,2},{7,3},{8,12},{9,13},{10,... | collective-permute-start | bytes 786440 | tf_op jit(solution)/shard_map/ppermute | solution.py:374
  50.5 0.7 copy-start.14
  58.4 0.7 copy-start.15
  143.9 22.5 %collective-permute-start.5 = (bf16[256,512]{1,0:T(8,128)(2,1)}, bf16[256,512]{1,0:T(8,128)(2,1)S(1)}, u32[]{:S(2)}, u32[]{:S(2)}) collective-permute-start(bf16[256,512]{1,0:T(8,128)(2,1)} %get-tuple-element.54), channel_id=1, source_target_pairs={{0,8},{1,9},{2,10},{3,11},{4,12},{5,13},{6,14},{7,15},{8,0},{9,1},... | collective-permute-start | bytes 786440 | tf_op jit(solution)/shard_map/ppermute | solution.py:374
  148.5 17.3 %collective-permute-start.7 = (f32[1,512]{1,0:T(1,128)}, f32[1,512]{1,0:T(1,128)S(1)}, u32[]{:S(2)}, u32[]{:S(2)}) collective-permute-start(f32[1,512]{1,0:T(1,128)} %get-tuple-element.56.fill_ref.refs_3_), channel_id=1, source_target_pairs={{0,8},{1,9},{2,10},{3,11},{4,12},{5,13},{6,14},{7,15},{8,0},{9,1},... | collective-permute-start | bytes 6152 | tf_op jit(solution)/shard_map/ppermute | solution.py:374
  149.9 22.8 %collective-permute-start.6 = (bf16[256,512]{1,0:T(8,128)(2,1)}, bf16[256,512]{1,0:T(8,128)(2,1)S(1)}, u32[]{:S(2)}, u32[]{:S(2)}) collective-permute-start(bf16[256,512]{1,0:T(8,128)(2,1)} %get-tuple-element.55), channel_id=1, source_target_pairs={{0,8},{1,9},{2,10},{3,11},{4,12},{5,13},{6,14},{7,15},{8,0},{9,1},... | collective-permute-start | bytes 786440 | tf_op jit(solution)/shard_map/ppermute | solution.py:374
  155.5 0.8 copy-start.6
  165.8 7.0 %copy-start.11 = (f32[1,512]{1,0:T(1,128)}, f32[1,512]{1,0:T(1,128)S(1)}, u32[]{:S(2)}) copy-start(f32[1,512]{1,0:T(1,128)S(1)} %collective-permute-done.7.refs_4_) | copy-start | bytes 6148
  166.4 0.7 copy-start.16
  172.8 0.7 copy-start.17
  173.5 31.7 %copy-start.5 = (s32[256,4]{1,0:T(8,128)S(1)}, s32[256,4]{1,0:T(8,128)}, u32[]{:S(2)}) copy-start(s32[256,4]{1,0:T(8,128)} %reshape.10.refs_18_) | copy-start | bytes 12292
  204.9 9.4 %collective-permute-start.8 = (bf16[256,512]{1,0:T(8,128)(2,1)}, bf16[256,512]{1,0:T(8,128)(2,1)S(1)}, u32[]{:S(2)}, u32[]{:S(2)}) collective-permute-start(bf16[256,512]{1,0:T(8,128)(2,1)} %get-tuple-element.65.x_ref.refs_14_), channel_id=1, source_target_pairs={{0,16},{1,17},{2,18},{3,19},{4,20},{5,21},{6,22},{7,23},{8,24},{9,... | collective-permute-start | bytes 786440 | tf_op jit(solution)/shard_map/ppermute | solution.py:374
  205.9 8.4 %collective-permute-start.9 = (f32[1,256]{1,0:T(1,128)}, f32[1,256]{1,0:T(1,128)S(1)}, u32[]{:S(2)}, u32[]{:S(2)}) collective-permute-start(f32[1,256]{1,0:T(1,128)} %get-tuple-element.66.fill_ref.refs_2_), channel_id=1, source_target_pairs={{0,16},{1,17},{2,18},{3,19},{4,20},{5,21},{6,22},{7,23},{8,24},{9,... | collective-permute-start | bytes 3080 | tf_op jit(solution)/shard_map/ppermute | solution.py:374
  214.2 0.5 copy-start.10
  214.2 0.7 copy-start.4

commit v2 on v1

v2 whole, which is shorter than its diff:
```python
import functools
import jax
import jax.numpy as jnp
from jax import lax
from jax.experimental import pallas as pl
from jax.experimental.pallas import tpu as pltpu
from jax.sharding import PartitionSpec as P

D = 512
HEAD = 64
HEADS = 8
VROWS = 80
LIMIT2 = 90.0**2
QSCALE = HEAD ** (-0.5) * 1.4426950408889634
NT = (((1,), (1,)), ((), ()))
TN = (((0,), (0,)), ((), ()))
BF = jnp.bfloat16
F32 = jnp.float32
ANY = pl.BlockSpec(memory_space=pl.ANY)
VLIMIT = 62 * 2**20


def dotf(a, b, dims=(((1,), (0,)), ((), ()))):
    return lax.dot_general(a, b, dims, preferred_element_type=F32)


def norm_rows(values, gain):
    wide = values.astype(F32)
    centre = jnp.mean(wide, axis=-1, keepdims=True)
    wide = wide - centre
    spread = jnp.mean(jnp.square(wide), axis=-1, keepdims=True)
    return (wide * lax.rsqrt(spread + 1e-05) * gain).astype(BF)


def to_column(row):
    eye = lax.broadcasted_iota(jnp.int32, (128, 128), 0) == lax.broadcasted_iota(
        jnp.int32, (128, 128), 1
    )
    parts = []
    for start in range(0, row.shape[1], 128):
        block = jnp.where(eye, row[:, start : start + 128], 0.0)
        parts.append(jnp.sum(block, axis=1, keepdims=True))
    return jnp.concatenate(parts, axis=0)


def head_select():
    lane = lax.broadcasted_iota(jnp.int32, (16, D), 1)
    head = lax.broadcasted_iota(jnp.int32, (16, D), 0)
    return jnp.where(lane // HEAD == head, 1.0, 0.0).astype(BF)


def head_peak(rows):
    wide = rows.astype(F32)
    sums = dotf(head_select(), (wide * wide).astype(BF), NT)
    return jnp.broadcast_to(jnp.max(sums, axis=1, keepdims=True), (16, 128))


def split_keys(keys, km_ref):
    low = lax.broadcasted_iota(jnp.int32, (1, 128), 1) < HEAD
    for pair in range(HEADS // 2):
        part = keys[:, pair * 128 : (pair + 1) * 128]
        km_ref[2 * pair] = jnp.where(low, part, jnp.zeros_like(part))
        km_ref[2 * pair + 1] = jnp.where(low, jnp.zeros_like(part), part)


def split_values(values_t, fill_row, va_ref):
    width = values_t.shape[1]
    first = lax.broadcasted_iota(jnp.int32, (16, width), 0) == 0
    ones = jnp.where(first, fill_row, 0.0).astype(BF)
    for head in range(HEADS):
        part = values_t[head * HEAD : (head + 1) * HEAD].astype(F32)
        va_ref[head, :HEAD, :] = (part * fill_row).astype(BF)
        va_ref[head, HEAD:, :] = ones


def attend(q_ref, km_ref, va_ref, o_ref, add_ref):
    count = km_ref.shape[1]
    blocks = [(start, min(256, count - start)) for start in range(0, count, 256)]

    def body(pair, carry):
        queries = q_ref[:, pl.ds(pl.multiple_of(pair * 128, 128), 128)]
        waiting = []

        def finish(head, block, scores, total):
            weights = jnp.exp2(scores).astype(BF)
            start, size = block
            values = va_ref[pair * 2 + head, :, start : start + size]
            part = dotf(values, weights)
            return part if total is None else total + part

        totals = [None, None]

        def drain():
            head, block, scores = waiting.pop(0)
            totals[head] = finish(head, block, scores, totals[head])
            if block == blocks[-1]:
                out = totals[head]
                if add_ref is not None:
                    out = out + add_ref[pair * 2 + head]
                o_ref[pair * 2 + head] = out

        for head in range(2):
            for block in blocks:
                start, size = block
                keys = km_ref[pair * 2 + head, start : start + size, :]
                waiting.append((head, block, dotf(keys, queries, NT)))
                if len(waiting) > 1:
                    drain()
        while waiting:
            drain()
        return carry

    lax.fori_loop(0, HEADS // 2, body, 0)


def project_kv(normed, kw, vw):
    keys = dotf(normed, kw.here[...]).astype(BF)
    values_t = dotf(vw.here[...], normed, (((0,), (1,)), ((), ()))).astype(BF)
    return keys, values_t


def local_kernel(level, rows, x, fill_src, gains, qw, kw, vw,
                 q, k, vt, o, qp, kp, km_ref, va_ref):
    normed = norm_rows(x.here[:rows, :], gains.here[level : level + 1, :])
    if level == 0:
        fill = fill_src.here[...].astype(F32)
        normed = normed * to_column(fill).astype(BF)
    else:
        fill = x.here[rows : rows + 1, :rows].astype(F32)
    queries = (dotf(normed, qw.here[...]) * QSCALE).astype(BF)
    q.ref[...] = queries
    q.flush()
    keys, values_t = project_kv(normed, kw, vw)
    k.ref[...] = keys
    vt.ref[...] = values_t
    k.flush()
    vt.flush()
    qp.ref[...] = head_peak(queries)
    kp.ref[...] = head_peak(keys)
    qp.flush()
    kp.flush()
    split_keys(keys, km_ref)
    split_values(values_t, fill, va_ref)
    attend(q.ref, km_ref, va_ref, o.ref, None)
    if level == 0:
        for head in range(HEADS):
            o.ref[head, HEAD : HEAD + 1, :] += 1.0 - fill
    else:
        prod = queries.astype(F32) * keys.astype(F32)
        high = prod.astype(BF)
        rest = (prod - high.astype(F32)).astype(BF)
        select = head_select()
        own = jnp.exp2(dotf(select, high, NT) + dotf(select, rest, NT))
        own = own * (1.0 - fill)
        for head in range(HEADS):
            weight = own[head : head + 1]
            part = values_t[head * HEAD : (head + 1) * HEAD].astype(F32)
            o.ref[head, :HEAD, :] += part * weight
            o.ref[head, HEAD : HEAD + 1, :] += weight
    o.flush()


def remote_kernel(level, at, x, fill, gains, kw, vw, q, kp_in, o_in, o, kp, km_ref, va_ref):
    rows = km_ref.shape[1]
    normed = norm_rows(x.here[:rows, :], gains.here[level : level + 1, :])
    keys, values_t = project_kv(normed, kw, vw)
    kp.ref[...] = jnp.maximum(kp_in.here[...], head_peak(keys))
    kp.flush()
    split_keys(keys, km_ref)
    split_values(values_t, fill.here[:, at : at + rows].astype(F32), va_ref)
    attend(q.here, km_ref, va_ref, o.ref, o_in.here)
    o.flush()


def exact_attend(level, q_ref, fills, chunk_refs, chunk_rows, gains, kw, vw,
                 k_loc, vt_loc, att_ref, xbuf, kf, vf):
    rows = q_ref.shape[0]
    pltpu.sync_copy(k_loc, kf.at[pl.ds(0, rows), :])
    pltpu.sync_copy(vt_loc, vf.at[:, pl.ds(0, rows)])
    at = rows
    for ref, count in zip(chunk_refs, chunk_rows):
        pltpu.sync_copy(ref.at[pl.ds(0, count), :], xbuf.at[pl.ds(0, count), :])
        normed = norm_rows(xbuf[:count, :], gains.here[level : level + 1, :])
        keys, values_t = project_kv(normed, kw, vw)
        kf[at : at + count, :] = keys
        vf[:, at : at + count] = values_t
        at += count
    total = 2 * rows
    low = lax.broadcasted_iota(jnp.int32, (1, 128), 1) < HEAD
    fill8 = jnp.broadcast_to(jnp.concatenate(fills, axis=1), (8, total)).astype(BF)
    width = 128

    def body(step, carry):
        pair = step // (rows // width)
        start = pl.multiple_of(step % (rows // width) * width, width)
        lanes = pl.ds(pl.multiple_of(pair * 128, 128), 128)
        queries = q_ref[pl.ds(start, width), lanes]
        keys = kf[:, lanes]
        mask = dotf(fill8, jnp.ones((8, width), BF), TN) > 0.5
        own = lax.broadcasted_iota(jnp.int32, (total, width), 0) == (
            lax.broadcasted_iota(jnp.int32, (total, width), 1) + start
        )
        allowed = mask | own
        for head in range(2):
            part = jnp.where(low if head == 0 else ~low, keys, jnp.zeros_like(keys))
            scores = jnp.where(allowed, dotf(part, queries, NT), -1e30)
            weights = jnp.exp2(scores - jnp.max(scores, axis=0, keepdims=True))
            weights = weights / jnp.sum(weights, axis=0, keepdims=True)
            first = pl.multiple_of(pair * 128 + head * HEAD, HEAD)
            values = vf[pl.ds(first, HEAD), :]
            att_ref[pl.ds(first, HEAD), pl.ds(start, width)] = dotf(
                values, weights.astype(BF)
            ).astype(BF)
        return carry

    lax.fori_loop(0, HEADS // 2 * (rows // width), body, 0)


def finish_attention(level, chunk_refs, chunk_rows, operands, scratch, fill, fills_far):
    last, gains, kw, vw, q, qp, kp, o_in, k_loc, vt_loc = operands
    att_ref, km_ref, va_ref, o_scr, xbuf, kf, vf = scratch
    rows = km_ref.shape[1]
    normed = norm_rows(last.here[:rows, :], gains.here[level : level + 1, :])
    keys, values_t = project_kv(normed, kw, vw)
    split_keys(keys, km_ref)
    split_values(values_t, fills_far[-1], va_ref)
    peak = jnp.maximum(kp.here[...], head_peak(keys)) * qp.here[...]
    attend(q.here, km_ref, va_ref, o_scr, o_in.here)
    for head in range(HEADS):
        scale = 1.0 / o_scr[head, HEAD : HEAD + 1, :]
        att_ref[head * HEAD : (head + 1) * HEAD, :] = (o_scr[head, :HEAD, :] * scale).astype(BF)
    inside = jnp.max(peak) <= LIMIT2

    @pl.when(jnp.logical_not(inside))
    def _():
        exact_attend(level, q.here, [fill] + fills_far, chunk_refs, chunk_rows, gains,
                     kw, vw, k_loc, vt_loc, att_ref, xbuf, kf, vf)

    return att_ref[...]


def finish0_kernel(counts, *refs):
    n = len(counts)
    chunks = refs[:n]
    (last, fill_ref, far_ref, gains, kw, vw, ow, q, qp, kp, o_in, k_loc, vt_loc, points, tree,
     y_out, x1_out) = refs[n : n + 17]
    scratch = refs[n + 17 :]
    fill = fill_ref.here[...].astype(F32)
    far = far_ref.here[...].astype(F32)
    fills_far, at = [], 0
    for count in counts:
        fills_far.append(far[:, at : at + count])
        at += count
    attended_t = finish_attention(
        0, chunks, counts, (last, gains, kw, vw, q, qp, kp, o_in, k_loc, vt_loc), scratch, fill,
        fills_far)
    x0 = points.here[...].astype(F32) * to_column(fill)
    y = (x0 + dotf(attended_t, ow.here[...], TN)).astype(BF)
    y_out.ref[...] = y
    y_out.flush()
    lanes = lax.broadcasted_iota(jnp.int32, (256, 1024), 1)
    f8 = jnp.broadcast_to(fill, (8, 1024)).astype(BF)
    order = tree.here
    fills = []
    for half in range(2):
        picked = (lanes == order[:, 2 * half : 2 * half + 1]) | (
            lanes == order[:, 2 * half + 1 : 2 * half + 2]
        )
        pool = jnp.where(picked, 0.5, 0.0).astype(BF)
        x1_out.ref[half * 256 : (half + 1) * 256, :] = dotf(pool, y).astype(BF)
        fills.append(jnp.where(dotf(f8, pool, NT)[:1] > 0.25, 1.0, 0.0))
    x1_out.ref[512:, :] = jnp.broadcast_to(jnp.concatenate(fills, axis=1), (16, D)).astype(BF)
    x1_out.flush()


def finish1_kernel(counts, far, last, gains, kw, vw, ow, q, qp, kp, o_in, k_loc, vt_loc, x,
                   y_out, x2_out, *scratch):
    fill = x.here[512:513, :].astype(F32)
    fills_far = [last.here[512:513, :].astype(F32)]
    attended_t = finish_attention(
        1, [far], counts, (last, gains, kw, vw, q, qp, kp, o_in, k_loc, vt_loc), scratch, fill,
        fills_far)
    y = (x.here[:512, :].astype(F32) + dotf(attended_t, ow.here[...], TN)).astype(BF)
    wide = y.astype(F32)
    x2_out.ref[:256, :] = ((wide[:256] + wide[256:]) * 0.5).astype(BF)
    f_next = jnp.maximum(fill[:, :256], fill[:, 256:])
    x2_out.ref[256:, :] = jnp.broadcast_to(
        jnp.concatenate([f_next, f_next], axis=1), (16, D)).astype(BF)
    x2_out.flush()
    y_out.ref[...] = y
    y_out.flush()


def finish2_kernel(counts, far, last, gains, kw, vw, ow, q, qp, kp, o_in, k_loc, vt_loc, x,
                   gm, hw, pw, y1, y0, tree, field, *scratch):
    fill = x.here[256:257, :256].astype(F32)
    fills_far = [last.here[256:257, :256].astype(F32)]
    attended_t = finish_attention(
        2, [far], counts, (last, gains, kw, vw, q, qp, kp, o_in, k_loc, vt_loc), scratch, fill,
        fills_far)
    y2 = (x.here[:256, :].astype(F32) + dotf(attended_t, ow.here[...], TN)).astype(BF)
    normed = norm_rows(y2, gm.here[...])
    hidden = jax.nn.gelu(dotf(normed, hw.here[...]), approximate=True).astype(BF)
    top = (y2.astype(F32) + dotf(hidden, pw.here[...])).astype(BF).astype(F32)
    up = [(y1.here[half * 256 : (half + 1) * 256, :].astype(F32) + top).astype(BF)
          for half in range(2)]
    rows = lax.broadcasted_iota(jnp.int32, (1024, 256), 0)
    total = y0.here[...].astype(F32)
    order = tree.here
    for half in range(2):
        picked = (rows == order[2 * half : 2 * half + 1, :]) | (
            rows == order[2 * half + 1 : 2 * half + 2, :]
        )
        total = total + dotf(jnp.where(picked, 1.0, 0.0).astype(BF), up[half])
    field.ref[...] = total.astype(BF)
    field.flush()


class Piece:
    def __init__(self, copy, ref):
        self.copy, self.ref = copy, ref

    @property
    def here(self):
        if self.copy is not None:
            self.copy.wait()
            self.copy = None
        return self.ref


class Result:
    def __init__(self, ref, copy):
        self.ref, self.copy = ref, copy

    def flush(self):
        self.copy.start()


def call(kernel, outs, args, raw=(), scratch=(), flops=0):
    arrays = [a[0] if isinstance(a, tuple) else a for a in args]
    levels = [a[1] if isinstance(a, tuple) else None for a in args]
    n, m = len(args), len(outs)
    moved = [i for i in range(n) if i not in raw]
    buffers = [
        pltpu.VMEM(a.shape if lv is None else a.shape[1:], a.dtype)
        for i, (a, lv) in enumerate(zip(arrays, levels)) if i not in raw
    ]

    def body(*refs):
        sources, targets = refs[:n], refs[n : n + m]
        held, rest = refs[n + m : n + m + len(moved)], refs[n + m + len(moved) :]
        results, rest = rest[:m], rest[m:]
        sem_in, sem_out, rest = rest[0], rest[1], rest[2:]
        operands = list(sources)
        for slot, i in enumerate(moved):
            source = sources[i] if levels[i] is None else sources[i].at[levels[i]]
            copy = pltpu.make_async_copy(source, held[slot], sem_in.at[slot])
            copy.start()
            operands[i] = Piece(copy, held[slot])
        products = [
            Result(results[i], pltpu.make_async_copy(results[i], targets[i], sem_out.at[i]))
            for i in range(m)
        ]
        kernel(*operands, *products, *rest)
        for operand in operands:
            if isinstance(operand, Piece):
                operand.here
        for product in products:
            product.copy.wait()

    nbytes = sum(a.size * a.dtype.itemsize for a in arrays) + sum(
        a.size * a.dtype.itemsize for a in outs)
    return pl.pallas_call(
        body,
        out_shape=outs,
        in_specs=[ANY] * n,
        out_specs=[ANY] * m,
        scratch_shapes=buffers + [pltpu.VMEM(o.shape, o.dtype) for o in outs]
        + [pltpu.SemaphoreType.DMA((len(moved),)), pltpu.SemaphoreType.DMA((m,))]
        + list(scratch),
        compiler_params=pltpu.CompilerParams(vmem_limit_bytes=VLIMIT),
        cost_estimate=pl.CostEstimate(flops=flops, bytes_accessed=nbytes, transcendentals=0),
    )(*arrays)


def shape(*dims, dtype=BF):
    return jax.ShapeDtypeStruct(dims, dtype)


def local_part(level, x, fill, gains, qw, kw, vw, rows):
    return call(
        functools.partial(local_kernel, level, rows),
        [shape(rows, D), shape(rows, D), shape(D, rows), shape(HEADS, VROWS, rows, dtype=F32),
         shape(16, 128, dtype=F32), shape(16, 128, dtype=F32)],
        [x, fill, gains, (qw, level), (kw, level), (vw, level)],
        scratch=[pltpu.VMEM((HEADS, rows, 128), BF), pltpu.VMEM((HEADS, VROWS, rows), BF)],
        flops=8 * rows * rows * 512 * 2,
    )


def remote_part(level, at, x, fill, gains, kw, vw, q, kp, o, count):
    rows = q.shape[0]
    return call(
        functools.partial(remote_kernel, level, at),
        [shape(HEADS, VROWS, rows, dtype=F32), shape(16, 128, dtype=F32)],
        [x, fill, gains, (kw, level), (vw, level), q, kp, o],
        scratch=[pltpu.VMEM((HEADS, count, 128), BF), pltpu.VMEM((HEADS, VROWS, count), BF)],
        flops=8 * rows * count * 512 * 2,
    )


def finish_part(kernel, counts, chunks, args, outs, rows, raw):
    n = len(counts)
    return call(
        functools.partial(kernel, counts),
        outs,
        list(chunks) + [chunks[-1]] + args,
        raw=set(range(n)) | {n + 1 + i for i in raw},
        scratch=[
            pltpu.VMEM((D, rows), BF),
            pltpu.VMEM((HEADS, counts[-1], 128), BF),
            pltpu.VMEM((HEADS, VROWS, counts[-1]), BF),
            pltpu.VMEM((HEADS, VROWS, rows), F32),
            pltpu.VMEM((max(counts), D), BF),
            pltpu.VMEM((2 * rows, D), BF),
            pltpu.VMEM((D, 2 * rows), BF),
        ],
        flops=8 * rows * counts[-1] * 512 * 2 + 4 * rows * D * D,
    )


def per_device(points, tree_order, present, gain_attn, query_weight, key_weight, value_weight,
               out_weight, gain_mlp, hidden_weight, proj_weight):
    size = lax.axis_size("leaf")

    def trade(value, bit):
        return lax.ppermute(value, "leaf", [(s, s ^ (1 << bit)) for s in range(size)])

    base = size.bit_length() - 1 - 3
    fill0 = present.reshape(1, 1024)
    far_fill = trade(fill0, base)
    counts0 = (384, 256, 256, 128)
    chunks, at = [], 0
    for i, count in enumerate(counts0):
        part = points[at : at + count]
        if i >= 2:
            part, _ = lax.optimization_barrier((part, chunks[i - 2]))
        chunks.append(trade(part, base))
        at += count
    tree4 = tree_order.reshape(256, 4)
    tree_rows = tree4.T

    def kvs(level):
        return [(key_weight, level), (value_weight, level)]

    q, k, vt, o, qp, kp = local_part(0, points, fill0, gain_attn, query_weight, key_weight,
                                     value_weight, 1024)
    at = 0
    for chunk, count in zip(chunks[:-1], counts0[:-1]):
        o, kp = remote_part(0, at, chunk, far_fill, gain_attn, key_weight, value_weight, q, kp, o,
                            count)
        at += count
    y0, x1 = finish_part(
        finish0_kernel, counts0, chunks,
        [fill0, far_fill, gain_attn, *kvs(0), (out_weight, 0), q, qp, kp, o, k, vt, points, tree4],
        [shape(1024, D), shape(528, D)], 1024, raw={10, 11})
    far1 = trade(x1, base + 1)
    q, k, vt, o, qp, kp = local_part(1, x1, fill0, gain_attn, query_weight, key_weight,
                                     value_weight, 512)
    y1, x2 = finish_part(
        finish1_kernel, (512,), [far1],
        [gain_attn, *kvs(1), (out_weight, 1), q, qp, kp, o, k, vt, x1],
        [shape(512, D), shape(272, D)], 512, raw={8, 9})
    far2 = trade(x2, base + 2)
    q, k, vt, o, qp, kp = local_part(2, x2, fill0, gain_attn, query_weight, key_weight,
                                     value_weight, 256)
    (field,) = finish_part(
        finish2_kernel, (256,), [far2],
        [gain_attn, *kvs(2), (out_weight, 2), q, qp, kp, o, k, vt, x2, gain_mlp.reshape(1, D),
         hidden_weight, proj_weight, y1, y0, tree_rows],
        [shape(1024, D)], 256, raw={8, 9})
    return field


def solution(mesh):
    placed = (
        P(("cloud", "leaf"), None),
        P(("cloud", "leaf")),
        P(("cloud", "leaf")),
        P(), P(), P(), P(), P(), P(), P(), P(),
    )
    return jax.shard_map(
        per_device,
        mesh=mesh,
        in_specs=placed,
        out_specs=P(("cloud", "leaf"), None),
        check_vma=False,
    )
```

time: 234 us -> 238 us (1.017)
  waiting for transfers between devices: 5.07 us -> 30.3 us
  local copies, waits for them, and re-layouts: 16.2 us -> 7.94 us
  starting transfers between devices: 23.3 us -> 15.5 us
  Pallas kernels: 188 us -> 183 us
    ppermute x10 -> x7, waiting for transfers between devices: 5.07 us -> 30.3 us  [trade(): return lax.ppermute(value, 'leaf', [(s, s ^ 1 << bit) for s in range(size)])]
    ppermute x10 -> x7, starting transfers between devices: 23.3 us -> 15.5 us  [trade(): return lax.ppermute(value, 'leaf', [(s, s ^ 1 << bit) for s in range(size)])]
    pallas_call x10 -> x9, Pallas kernels: 188 us -> 183 us  [call(): pl.pallas_call(body, out_shape=outs, in_specs=[ANY] * n, out_specs=[ANY]...]
    squeeze x3 -> x0, local copies, waits for them, and re-layouts: 4.16 us -> none  [the longest x1 1.74 us: per_device(): value_weight[2]]
    unnamed x39 -> x18, local copies, waits for them, and re-layouts: 6.52 us -> 3.49 us
  transfers between devices with their start and end apart: 10 -> 7, of which waited for: 2 -> 4; matrix products, arithmetic and copies ran while one was open for 4% -> 2% of each run, Pallas kernels for 24% -> 21%
where the time goes in v2:
time: 238 us; the launch traced here: 237 us
  Pallas kernels  183 us (77%)
  waiting for transfers between devices  30.3 us (13%)
  starting transfers between devices  15.5 us (7%)
  local copies, waits for them, and re-layouts  7.94 us (3%)
    pallas_call x9, Pallas kernels, call(): pl.pallas_call(body, out_shape=outs, in_specs=[ANY] * n, out_specs=[ANY]...  183 us
    ppermute x7, waiting for transfers between devices, trade(): return lax.ppermute(value, 'leaf', [(s, s ^ 1 << bit) for s in range(size)])  30.3 us
    ppermute x7, starting transfers between devices, trade(): return lax.ppermute(value, 'leaf', [(s, s ^ 1 << bit) for s in range(size)])  15.5 us
  transfers between devices with their start and end apart: 7, of which 4 were waited for; matrix products, arithmetic and copies ran while one was open for 2% of the time, Pallas kernels for 21%

profile of v2, /device:TPU:18, one launch (start us, length us, event | category | flops | bytes accessed | tf_op | source)
XLA Modules:
  0.0 237.5 jit_solution(17988354833317651385)
XLA Ops:
  0.0 3.3 %collective-permute-start.4 = (s32[1,1024]{1,0:T(1,128)}, s32[1,1024]{1,0:T(1,128)S(1)}, u32[]{:S(2)}, u32[]{:S(2)}) collective-permute-start(s32[1,1024]{1,0:T(1,128)} %bitcast.3), channel_id=1, source_target_pairs={{0,4},{1,5},{2,6},{3,7},{4,0},{5,1},{6,2},{7,3},{8,12},{9,13},{10,... | collective-permute-start | bytes 12296 | tf_op jit(solution)/shard_map/ppermute | solution.py:437
  3.3 1.0 slice.12
  4.3 0.1 collective-permute-start
  4.4 1.1 fusion
  5.5 0.0 copy-start.7
  5.5 3.0 %collective-permute-start.1 = (bf16[256,512]{1,0:T(8,128)(2,1)S(1)}, bf16[256,512]{1,0:T(8,128)(2,1)S(1)}, u32[]{:S(2)}, u32[]{:S(2)}) collective-permute-start(bf16[256,512]{1,0:T(8,128)(2,1)S(1)} %get-tuple-element.66), channel_id=1, source_target_pairs={{0,4},{1,5},{2,6},{3,7},{4,0},{5,1},{6,2},{7,3},{8,12},{9,13},{10,... | collective-permute-start | bytes 786440 | tf_op jit(solution)/shard_map/ppermute | solution.py:437
  8.5 15.1 %shard_map.109 = (bf16[1024,512]{1,0:T(8,128)(2,1)}, bf16[1024,512]{1,0:T(8,128)(2,1)}, bf16[512,1024]{1,0:T(8,128)(2,1)}, f32[8,80,1024]{2,1,0:T(8,128)}, f32[16,128]{1,0:T(8,128)}, /*index=5*/f32[16,128]{1,0:T(8,128)}) custom-call(bf16[1024,512]{1,0:T(8,128)(2,1)} %refs_17_.1, s32[1,1024]{1,0:T(1,128)} %bitcast.4, f32[3,512]{1,0:T(4,128)} %refs_2_.15, ...), custom_call_target="tpu_custom_call" | custom-call | flops 8589934592 | bytes 11560960 | tf_op jit(solution)/shard_map/pallas_call | solution.py:373
  23.6 0.9 slice.15
  24.5 0.0 copy-done.7
  24.5 0.8 reshape.10.refs_18_
  25.3 10.2 %collective-permute-done.1.refs_0_.refs_1_ = bf16[256,512]{1,0:T(8,128)(2,1)S(1)} collective-permute-done((bf16[256,512]{1,0:T(8,128)(2,1)S(1)}, bf16[256,512]{1,0:T(8,128)(2,1)S(1)}, u32[]{:S(2)}, u32[]{:S(2)}) %collective-permute-start.1) | collective-permute-done | bytes 262176 | tf_op jit(solution)/shard_map/ppermute | solution.py:437
  35.5 0.0 copy-start.4
  35.5 0.0 collective-permute-start.3
  35.5 0.0 collective-permute-done.refs_0_
  35.5 0.0 copy-start.3
  35.5 2.9 %collective-permute-start.2 = (bf16[256,512]{1,0:T(8,128)(2,1)S(1)}, bf16[256,512]{1,0:T(8,128)(2,1)S(1)}, u32[]{:S(2)}, u32[]{:S(2)}) collective-permute-start(bf16[256,512]{1,0:T(8,128)(2,1)S(1)} %get-tuple-element.35), channel_id=1, source_target_pairs={{0,4},{1,5},{2,6},{3,7},{4,0},{5,1},{6,2},{7,3},{8,12},{9,13},{10,... | collective-permute-start | bytes 786440 | tf_op jit(solution)/shard_map/ppermute | solution.py:437
  38.5 0.0 collective-permute-done.4.refs_1_.refs_6_
  38.5 0.0 copy-start.6
  38.5 0.0 copy-done.3
  38.5 0.6 copy-done.6
  39.1 8.2 %shard_map.110 = (f32[8,80,1024]{2,1,0:T(8,128)}, f32[16,128]{1,0:T(8,128)}) custom-call(bf16[384,512]{1,0:T(8,128)(2,1)} %copy-done.3, s32[1,1024]{1,0:T(1,128)} %copy-done.6, f32[3,512]{1,0:T(4,128)} %refs_2_.15, bf16[3,512,512]{2,1,0:T(8,128)(2,1)} %refs_3_.15, bf16[3,512,512]{2,1,0:T(8,128)(2,1)} %refs_4_.15, ...), custom_call_target="tpu_custom_call" | custom-call | flops 3221225472 | bytes 9857024 | tf_op jit(solution)/shard_map/pallas_call | solution.py:373
  47.2 0.0 copy-done.4
  47.2 6.6 %shard_map.111 = (f32[8,80,1024]{2,1,0:T(8,128)}, f32[16,128]{1,0:T(8,128)}) custom-call(bf16[256,512]{1,0:T(8,128)(2,1)} %copy-done.4, s32[1,1024]{1,0:T(1,128)} %copy-done.6, f32[3,512]{1,0:T(4,128)} %refs_2_.15, bf16[3,512,512]{2,1,0:T(8,128)(2,1)} %refs_3_.15, bf16[3,512,512]{2,1,0:T(8,128)(2,1)} %refs_4_.15, ...), custom_call_target="tpu_custom_call" | custom-call | flops 2147483648 | bytes 9725952 | tf_op jit(solution)/shard_map/pallas_call | solution.py:373
  53.9 0.7 collective-permute-done.2.refs_0_.refs_2_
  54.5 0.0 copy-start.5
  54.5 0.7 copy-done.5
  55.2 6.5 %shard_map.112 = (f32[8,80,1024]{2,1,0:T(8,128)}, f32[16,128]{1,0:T(8,128)}) custom-call(bf16[256,512]{1,0:T(8,128)(2,1)} %copy-done.5, s32[1,1024]{1,0:T(1,128)} %copy-done.6, f32[3,512]{1,0:T(4,128)} %refs_2_.15, bf16[3,512,512]{2,1,0:T(8,128)(2,1)} %refs_3_.15, bf16[3,512,512]{2,1,0:T(8,128)(2,1)} %refs_4_.15, ...), custom_call_target="tpu_custom_call" | custom-call | flops 2147483648 | bytes 9725952 | tf_op jit(solution)/shard_map/pallas_call | solution.py:373
  61.8 0.0 collective-permute-done.3.refs_3_.refs_4_
  61.8 0.0 copy-start.2
  61.8 0.6 copy-done.2
  62.4 83.1 %shard_map.113 = (bf16[1024,512]{1,0:T(8,128)(2,1)}, bf16[528,512]{1,0:T(8,128)(2,1)}) custom-call(bf16[384,512]{1,0:T(8,128)(2,1)} %copy-done.3, bf16[256,512]{1,0:T(8,128)(2,1)} %copy-done.4, bf16[256,512]{1,0:T(8,128)(2,1)} %copy-done.5, bf16[128,512]{1,0:T(8,128)(2,1)} %copy-done.2, bf16[128,512]{1,0:T(8,128)(2,1)} %copy-done.2, s32[1,1024]{1,0:T(1,128)} %bitcast.5, ...), custom_call_target="tpu_custom_call" | custom-call | flops 2147483648 | bytes 14338048 | tf_op jit(solution)/shard_map/pallas_call | solution.py:373
  145.6 5.8 %collective-permute-start.5 = (bf16[528,512]{1,0:T(8,128)(2,1)}, bf16[528,512]{1,0:T(8,128)(2,1)S(1)}, u32[]{:S(2)}, u32[]{:S(2)}) collective-permute-start(bf16[528,512]{1,0:T(8,128)(2,1)} %get-tuple-element.49.refs_0_.refs_12_), channel_id=1, source_target_pairs={{0,8},{1,9},{2,10},{3,11},{4,12},{5,13},{6,14},{7,15},{8,0},{9,1},... | collective-permute-start | bytes 1622024 | tf_op jit(solution)/shard_map/ppermute | solution.py:437
  151.4 8.2 %shard_map.114 = (bf16[512,512]{1,0:T(8,128)(2,1)}, bf16[512,512]{1,0:T(8,128)(2,1)}, bf16[512,512]{1,0:T(8,128)(2,1)}, f32[8,80,512]{2,1,0:T(8,128)}, f32[16,128]{1,0:T(8,128)}, /*index=5*/f32[16,128]{1,0:T(8,128)}) custom-call(bf16[528,512]{1,0:T(8,128)(2,1)} %get-tuple-element.49.refs_0_.refs_12_, s32[1,1024]{1,0:T(1,128)} %bitcast.6, f32[3,512]{1,0:T(4,128)} %refs_2_.15, ...), custom_call_target="tpu_custom_call" | custom-call | flops 2147483648 | bytes 8169472 | tf_op jit(solution)/shard_map/pallas_call | solution.py:373
  159.6 16.3 %collective-permute-done.5.refs_0_.refs_1_ = bf16[528,512]{1,0:T(8,128)(2,1)S(1)} collective-permute-done((bf16[528,512]{1,0:T(8,128)(2,1)}, bf16[528,512]{1,0:T(8,128)(2,1)S(1)}, u32[]{:S(2)}, u32[]{:S(2)}) %collective-permute-start.5) | collective-permute-done | bytes 540704 | tf_op jit(solution)/shard_map/ppermute | solution.py:437
  175.9 0.0 copy-start.8
  175.9 0.8 copy-done.8
  176.7 0.0 copy-start
  176.7 32.5 %shard_map.115 = (bf16[512,512]{1,0:T(8,128)(2,1)}, bf16[272,512]{1,0:T(8,128)(2,1)}) custom-call(bf16[528,512]{1,0:T(8,128)(2,1)} %copy-done.8, bf16[528,512]{1,0:T(8,128)(2,1)} %copy-done.8, f32[3,512]{1,0:T(4,128)} %refs_2_.15, bf16[3,512,512]{2,1,0:T(8,128)(2,1)} %refs_3_.15, bf16[3,512,512]{2,1,0:T(8,128)(2,1)} %refs_4_.15, ...), custom_call_target="tpu_custom_call" | custom-call | flops 2684354560 | bytes 10049536 | tf_op jit(solution)/shard_map/pallas_call | solution.py:373
  209.3 0.4 collective-permute-start.6
  209.7 0.0 copy-done
  209.7 0.7 copy.13
  210.4 5.2 %shard_map.116 = (bf16[256,512]{1,0:T(8,128)(2,1)}, bf16[256,512]{1,0:T(8,128)(2,1)}, bf16[512,256]{1,0:T(8,128)(2,1)}, f32[8,80,256]{2,1,0:T(8,128)}, f32[16,128]{1,0:T(8,128)}, /*index=5*/f32[16,128]{1,0:T(8,128)}) custom-call(bf16[272,512]{1,0:T(8,128)(2,1)} %get-tuple-element.56.refs_0_.refs_12_, s32[1,1024]{1,0:T(1,128)} %bitcast.7, f32[3,512]{1,0:T(4,128)} %refs_2_.15, ...), custom_call_target="tpu_custom_call" | custom-call | flops 536870912 | bytes 6465536 | tf_op jit(solution)/shard_map/pallas_call | solution.py:373
  215.6 3.1 %collective-permute-done.6.refs_0_.refs_1_ = bf16[272,512]{1,0:T(8,128)(2,1)S(1)} collective-permute-done((bf16[272,512]{1,0:T(8,128)(2,1)}, bf16[272,512]{1,0:T(8,128)(2,1)S(1)}, u32[]{:S(2)}, u32[]{:S(2)}) %collective-permute-start.6) | collective-permute-done | bytes 278560 | tf_op jit(solution)/shard_map/ppermute | solution.py:437
  218.7 0.0 copy-start.1
  218.7 0.7 copy-done.1
  219.4 17.8 %shard_map.117 = bf16[1024,512]{1,0:T(8,128)(2,1)} custom-call(bf16[272,512]{1,0:T(8,128)(2,1)} %copy-done.1, bf16[272,512]{1,0:T(8,128)(2,1)} %copy-done.1, f32[3,512]{1,0:T(4,128)} %refs_2_.15, bf16[3,512,512]{2,1,0:T(8,128)(2,1)} %refs_3_.15, bf16[3,512,512]{2,1,0:T(8,128)(2,1)} %refs_4_.15, bf16[3,512,512]{2,1,0:T(8,128)(2,1)} %refs_5_.9, ...), custom_call_target="tpu_custom_call" | custom-call | flops 805306368 | bytes 13840384 | tf_op jit(solution)/shard_map/pallas_call | solution.py:373
Async XLA Ops:
  0.0 38.5 %collective-permute-start.4 = (s32[1,1024]{1,0:T(1,128)}, s32[1,1024]{1,0:T(1,128)S(1)}, u32[]{:S(2)}, u32[]{:S(2)}) collective-permute-start(s32[1,1024]{1,0:T(1,128)} %bitcast.3), channel_id=1, source_target_pairs={{0,4},{1,5},{2,6},{3,7},{4,0},{5,1},{6,2},{7,3},{8,12},{9,13},{10,... | collective-permute-start | bytes 12296 | tf_op jit(solution)/shard_map/ppermute | solution.py:437
  4.3 31.2 %collective-permute-start = (bf16[384,512]{1,0:T(8,128)(2,1)S(1)}, bf16[384,512]{1,0:T(8,128)(2,1)S(1)}, u32[]{:S(2)}, u32[]{:S(2)}) collective-permute-start(bf16[384,512]{1,0:T(8,128)(2,1)S(1)} %slice.12), channel_id=1, source_target_pairs={{0,4},{1,5},{2,6},{3,7},{4,0},{5,1},{6,2},{7,3},{8,12},{9,13},{10,... | collective-permute-start | bytes 1179656 | tf_op jit(solution)/shard_map/ppermute | solution.py:437
  5.5 19.0 %copy-start.7 = (s32[1024]{0:T(1024)S(1)}, s32[1024]{0:T(1024)}, u32[]{:S(2)}) copy-start(s32[1024]{0:T(1024)} %param.12) | copy-start | bytes 12292
  5.5 30.0 %collective-permute-start.1 = (bf16[256,512]{1,0:T(8,128)(2,1)S(1)}, bf16[256,512]{1,0:T(8,128)(2,1)S(1)}, u32[]{:S(2)}, u32[]{:S(2)}) collective-permute-start(bf16[256,512]{1,0:T(8,128)(2,1)S(1)} %get-tuple-element.66), channel_id=1, source_target_pairs={{0,4},{1,5},{2,6},{3,7},{4,0},{5,1},{6,2},{7,3},{8,12},{9,13},{10,... | collective-permute-start | bytes 786440 | tf_op jit(solution)/shard_map/ppermute | solution.py:437
  35.5 11.7 %copy-start.4 = (bf16[256,512]{1,0:T(8,128)(2,1)}, bf16[256,512]{1,0:T(8,128)(2,1)S(1)}, u32[]{:S(2)}) copy-start(bf16[256,512]{1,0:T(8,128)(2,1)S(1)} %collective-permute-done.1.refs_0_.refs_1_) | copy-start | bytes 786436
  35.5 26.3 %collective-permute-start.3 = (bf16[128,512]{1,0:T(8,128)(2,1)S(1)}, bf16[128,512]{1,0:T(8,128)(2,1)S(1)}, u32[]{:S(2)}, u32[]{:S(2)}) collective-permute-start(bf16[128,512]{1,0:T(8,128)(2,1)S(1)} %slice.15), channel_id=1, source_target_pairs={{0,4},{1,5},{2,6},{3,7},{4,0},{5,1},{6,2},{7,3},{8,12},{9,13},{10,... | collective-permute-start | bytes 393224 | tf_op jit(solution)/shard_map/ppermute | solution.py:437
  35.5 2.9 %copy-start.3 = (bf16[384,512]{1,0:T(8,128)(2,1)}, bf16[384,512]{1,0:T(8,128)(2,1)S(1)}, u32[]{:S(2)}) copy-start(bf16[384,512]{1,0:T(8,128)(2,1)S(1)} %collective-permute-done.refs_0_) | copy-start | bytes 1179652
  35.5 19.0 %collective-permute-start.2 = (bf16[256,512]{1,0:T(8,128)(2,1)S(1)}, bf16[256,512]{1,0:T(8,128)(2,1)S(1)}, u32[]{:S(2)}, u32[]{:S(2)}) collective-permute-start(bf16[256,512]{1,0:T(8,128)(2,1)S(1)} %get-tuple-element.35), channel_id=1, source_target_pairs={{0,4},{1,5},{2,6},{3,7},{4,0},{5,1},{6,2},{7,3},{8,12},{9,13},{10,... | collective-permute-start | bytes 786440 | tf_op jit(solution)/shard_map/ppermute | solution.py:437
  38.5 0.6 copy-start.6
  54.5 0.7 copy-start.5
  61.8 0.7 copy-start.2
  145.6 30.3 %collective-permute-start.5 = (bf16[528,512]{1,0:T(8,128)(2,1)}, bf16[528,512]{1,0:T(8,128)(2,1)S(1)}, u32[]{:S(2)}, u32[]{:S(2)}) collective-permute-start(bf16[528,512]{1,0:T(8,128)(2,1)} %get-tuple-element.49.refs_0_.refs_12_), channel_id=1, source_target_pairs={{0,8},{1,9},{2,10},{3,11},{4,12},{5,13},{6,14},{7,15},{8,0},{9,1},... | collective-permute-start | bytes 1622024 | tf_op jit(solution)/shard_map/ppermute | solution.py:437
  175.9 0.8 copy-start.8
  176.7 33.0 %copy-start = (s32[256,4]{1,0:T(8,128)S(1)}, s32[256,4]{1,0:T(8,128)}, u32[]{:S(2)}) copy-start(s32[256,4]{1,0:T(8,128)} %reshape.10.refs_18_) | copy-start | bytes 12292
  209.3 9.4 %collective-permute-start.6 = (bf16[272,512]{1,0:T(8,128)(2,1)}, bf16[272,512]{1,0:T(8,128)(2,1)S(1)}, u32[]{:S(2)}, u32[]{:S(2)}) collective-permute-start(bf16[272,512]{1,0:T(8,128)(2,1)} %get-tuple-element.56.refs_0_.refs_12_), channel_id=1, source_target_pairs={{0,16},{1,17},{2,18},{3,19},{4,20},{5,21},{6,22},{7,23},{8,24},{9,... | collective-permute-start | bytes 835592 | tf_op jit(solution)/shard_map/ppermute | solution.py:437
  218.7 0.7 copy-start.1
